TPU v7x, 128 devices: a whole 4x4x4 slice. The times are simulated.
128 devices in a mesh: stream: 32 (over z, x, core), span: 4 (over y).
Axes of the slice: x: 4, y: 4, z: 4, core: 2. Of those that a mesh axis runs over, the one named last changes fastest.
Arguments:
- q_now: float32 [5, 512, 128, 128], P(None, 'stream', 'span'), may hold values from -4 to 4
- q_prev: float32 [5, 512, 128, 128], P(None, 'stream', 'span'), may hold values from -4 to 4
- jacobians: float32 [3, 5, 5], replicated, may hold values from -2.5 to 2.5
- fractions: float32 [3, 128, 4096], P(None, ('stream', 'span')), may hold values from 0 to 0.9
- send_blocks: int32 [128, 4096], P(('stream', 'span')), may hold values from -1 to 8191, as said below
- recv_blocks: int32 [128, 4096], P(('stream', 'span')), may hold values from -1 to 8191, as said below
Outputs:
- q_next: float32 [5, 512, 128, 128], P(None, 'stream', 'span')
Inputs may be any that keep to these rules, and one draw needn't show every extreme that they name: In each row of send_blocks, the 32 slots to one destination hold valid brick indices first and -1 after them; a device sends only to devices whose streamwise rank differs from its own by at most 2, and to the device whose rank differs from its own by 64, which always receives exactly 32 valid slots from it; the busiest receivers get several times the mean. recv_blocks[r, s * 32 + k] is -1 exactly where send_blocks[s, r * 32 + k] is; the valid entries of one row are distinct.
All inputs are finite; a program needn't handle non-finite values.
Results may differ from a plain program's by a relative error of at most 0.0003.
Values sent between devices are 32-bit elements; how exact they have to be, the bound alone decides.
A program may use at most 192 MiB of HBM per device.

v0:
```python
import functools

import jax
import jax.numpy as jnp
from jax import lax
from jax.experimental import pallas as pl
from jax.experimental.pallas import tpu as pltpu
from jax.sharding import PartitionSpec as P

MESH = pl.DeviceIdType.MESH
F32 = jnp.float32
VARS = 5
CHANS = 10
SLOT = 32
REACH = 2
GROUPS = 2 * REACH + 1
CX, CY, CZ = 16, 32, 128
BX, BY = CX // 2, CY // 2
ROW = 2 * CHANS
BRICK = 2 * ROW
ROWS = BX * CY * ROW
PAD = 8
WY = CY + 2 * PAD
NEAR, FAR = 2, 5
SCALE = 0.6 / 1024.0
TAPS = (-252.0, 210.0, -120.0, 45.0, -10.0, 1.0)


def lanes(shape):
    return lax.broadcasted_iota(jnp.int32, shape, len(shape) - 1)


def window_start(i, n_stream):
    return jnp.minimum(jnp.maximum(i - REACH, 0), n_stream - GROUPS)


def pack_kernel(n_stream, n_span, send_hbm, now_ref, prev_ref, packed_ref, sending_ref, picks, sem):
    i = lax.axis_index("stream")
    j = lax.axis_index("span")
    first = window_start(i, n_stream)
    far = lax.rem(i + n_stream // 2, n_stream)
    near_count = GROUPS * n_span
    copies = [
        pltpu.make_async_copy(send_hbm.at[pl.ds(first, GROUPS)], picks.at[pl.ds(0, GROUPS)], sem.at[0]),
        pltpu.make_async_copy(send_hbm.at[pl.ds(far, 1)], picks.at[pl.ds(GROUPS, 1)], sem.at[1]),
    ]
    for copy in copies:
        copy.start()

    def relayout(xb, carry):
        for dx in range(2):
            for tile in range(CY // 8):
                base = xb * (CY * ROW) + tile * 8 * ROW + dx * CHANS
                for c in range(VARS):
                    packed_ref[pl.ds(base + c, 8, ROW), :] = now_ref[c, 2 * xb + dx, tile * 8:tile * 8 + 8, :]
                    packed_ref[pl.ds(base + VARS + c, 8, ROW), :] = prev_ref[c, 2 * xb + dx, tile * 8:tile * 8 + 8, :]
        return carry

    lax.fori_loop(0, BX, relayout, 0)
    for copy in copies:
        copy.wait()
    half = lanes((ROW, 128)) < 64
    pair = lanes((BRICK, 128)) // 2
    chunk = 8

    def pack(p, carry):
        row = p // n_span
        start = jnp.where(p < near_count, lax.rem(p, n_span), j) * SLOT

        def some(head, total):
            def more(total):
                for k in range(head, head + chunk):
                    brick = jnp.maximum(picks[row, 0, start + k], 0)
                    base = pl.multiple_of((brick >> 6) * BRICK, 8)
                    shift = (2 * k - 2 * (brick & 63)) & 127
                    moved = pltpu.roll(packed_ref[pl.ds(base, BRICK), :], shift, 1)
                    total = jnp.where(pair == k, moved, total)
                return total
            return lax.cond(picks[row, 0, start + head] >= 0, more, lambda total: total, total)

        total = jnp.zeros((BRICK, 128), F32)
        for head in range(0, SLOT, chunk):
            total = some(head, total)
        sending_ref[p] = jnp.where(half, total[:ROW], pltpu.roll(total[ROW:], 64, 1))
        return carry

    lax.fori_loop(0, near_count + 1, pack, 0)


def exchange_kernel(n_stream, n_span, frac_ref, sending, fresh_ref, arrived, send_sem, recv_sem):
    i = lax.axis_index("stream")
    j = lax.axis_index("span")
    first = window_start(i, n_stream)
    far = lax.rem(i + n_stream // 2, n_stream)
    near_count = GROUPS * n_span
    far_slot = near_count

    def is_partner(g, jp):
        t = first + g
        return (t >= i - REACH) & (t <= i + REACH) & ((t != i) | (jp != j))

    barrier = pltpu.get_barrier_semaphore()
    for g in range(GROUPS):
        for jp in range(n_span):
            @pl.when(is_partner(g, jp))
            def _():
                pl.semaphore_signal(barrier, inc=1, device_id=(first + g, jp), device_id_type=MESH)
    pl.semaphore_signal(barrier, inc=1, device_id=(far, j), device_id_type=MESH)

    rows_near = jnp.minimum(i + REACH, n_stream - 1) - jnp.maximum(i - REACH, 0) + 1
    pl.semaphore_wait(barrier, rows_near * n_span)

    def far_copy():
        return pltpu.make_async_remote_copy(
            src_ref=sending.at[far_slot], dst_ref=arrived.at[far_slot],
            send_sem=send_sem.at[far_slot], recv_sem=recv_sem.at[far_slot],
            device_id=(far, j), device_id_type=MESH,
        )

    far_copy().start()

    def near_copy(p):
        g = p // n_span
        jp = lax.rem(p, n_span)
        t = first + g
        slot = (i - window_start(t, n_stream)) * n_span + j
        slot = jnp.minimum(jnp.maximum(slot, 0), near_count - 1)
        return pltpu.make_async_remote_copy(
            src_ref=sending.at[p], dst_ref=arrived.at[slot],
            send_sem=send_sem.at[p], recv_sem=recv_sem.at[slot],
            device_id=(t, jp), device_id_type=MESH,
        )

    def arrival(p):
        return pltpu.make_async_remote_copy(
            src_ref=sending.at[p], dst_ref=arrived.at[p],
            send_sem=send_sem.at[p], recv_sem=recv_sem.at[p],
            device_id=(first + p // n_span, lax.rem(p, n_span)), device_id_type=MESH,
        )

    def send(p, carry):
        g = p // n_span
        jp = lax.rem(p, n_span)
        t = first + g

        @pl.when(is_partner(g, jp))
        def _():
            near_copy(p).start()

        return carry

    lax.fori_loop(0, near_count, send, 0)
    own = (i - first) * n_span + j
    arrived[own] = sending[own]

    near_frac = [frac_ref[d, pl.ds(first, GROUPS), :] for d in range(3)]
    far_frac = [frac_ref[d, pl.ds(far, 1), :] for d in range(3)]
    table = jnp.concatenate([part for d in range(3) for part in (near_frac[d], far_frac[d])], 0)

    def spread(which):
        source = lax.broadcasted_iota(jnp.int32, (128, 128), 0)
        wanted = which * SLOT + lax.rem(lanes((128, 128)), 64) // 2
        chosen = jnp.where(source == wanted, 1.0, 0.0).astype(F32)
        return jnp.dot(table, chosen, precision=lax.Precision.HIGHEST, preferred_element_type=F32)

    spreads = [spread(jp) for jp in range(n_span)]
    far_spread = spread(j)
    even = lanes((CHANS, 128)) % 2 == 0
    low_half = lanes((CHANS, 128)) < 64

    def finish(p, fx, fy, fz):
        block = arrived[p]
        upper = block[CHANS:]
        lower = (1.0 - fx) * block[:CHANS] + fx * upper
        done = []
        for v in (lower, upper):
            v = jnp.where(low_half, (1.0 - fy) * v + fy * pltpu.roll(v, 64, 1), v)
            v = jnp.where(even, (1.0 - fz) * v + fz * pltpu.roll(v, 127, 1), v)
            done.append(v)
        both = jnp.concatenate(done, 0)
        fresh_ref[p, 0:ROW, :] = both
        fresh_ref[p, ROW:BRICK, :] = pltpu.roll(both, 64, 1)

    for p in range(near_count):
        g, jp = p // n_span, p % n_span

        @pl.when(is_partner(g, jp))
        def _():
            arrival(p).wait()

        finish(p, *(spreads[jp][6 * d + g:6 * d + g + 1] for d in range(3)))
    far_copy().wait()
    finish(far_slot, *(far_spread[6 * d + GROUPS:6 * d + GROUPS + 1] for d in range(3)))


def place_kernel(n_stream, n_span, recv_hbm, packed_hbm, fresh_ref, now_ref, prev_ref, targets, work, sem):
    i = lax.axis_index("stream")
    j = lax.axis_index("span")
    first = window_start(i, n_stream)
    far = lax.rem(i + n_stream // 2, n_stream)
    near_count = GROUPS * n_span
    copies = [
        pltpu.make_async_copy(recv_hbm.at[pl.ds(first, GROUPS)], targets.at[pl.ds(0, GROUPS)], sem.at[0]),
        pltpu.make_async_copy(recv_hbm.at[pl.ds(far, 1)], targets.at[pl.ds(GROUPS, 1)], sem.at[1]),
        pltpu.make_async_copy(packed_hbm, work, sem.at[2]),
    ]
    for copy in copies:
        copy.start()
    for copy in copies:
        copy.wait()
    pair = lanes((BRICK, 128)) // 2
    chunk = 8

    def put(p, carry):
        row = p // n_span
        start = jnp.where(p < near_count, lax.rem(p, n_span), j) * SLOT
        for head in range(0, SLOT, chunk):
            @pl.when(targets[row, 0, start + head] >= 0)
            def _():
                block = fresh_ref[p]
                for k in range(head, head + chunk):
                    target = targets[row, 0, start + k]
                    brick = jnp.maximum(target, 0)
                    column = lax.rem(brick, 64)
                    base = pl.multiple_of((brick // 64) * BRICK, 8)
                    shift = lax.rem(2 * column - 2 * k + 128, 128)
                    moved = pltpu.roll(block, shift, 1)
                    mark = jnp.where(target >= 0, column, -1)
                    pltpu.store(work.at[pl.ds(base, BRICK), :], moved, mask=pair == mark)
        return carry

    lax.fori_loop(0, near_count + 1, put, 0)

    def relayout(xb, carry):
        for dx in range(2):
            for tile in range(CY // 8):
                base = xb * (CY * ROW) + tile * 8 * ROW + dx * CHANS
                for c in range(VARS):
                    now_ref[c, 2 * xb + dx, tile * 8:tile * 8 + 8, :] = work[pl.ds(base + c, 8, ROW), :]
                    prev_ref[c, 2 * xb + dx, tile * 8:tile * 8 + 8, :] = work[pl.ds(base + VARS + c, 8, ROW), :]
        return carry

    lax.fori_loop(0, BX, relayout, 0)


def band(entries):
    source = lax.rem(lax.broadcasted_iota(jnp.int32, (2 * CZ, CZ), 0), CZ)
    away = source - lanes((2 * CZ, CZ))
    total = jnp.zeros((2 * CZ, CZ), F32)
    for offset, weight in entries:
        total = jnp.where(away == offset, weight, total)
    return total.astype(jnp.bfloat16)


def along_z(values, matrix):
    high = values.astype(jnp.bfloat16)
    low = (values - high.astype(F32)).astype(jnp.bfloat16)
    both = jnp.concatenate([high, low], 1)
    return jnp.dot(both, matrix, preferred_element_type=F32)


def advance_kernel(
    n_stream, n_span, jac, q_hbm, old_ref, out_ref,
    wide, pre, y_near_out, y_near_in, y_far_out, y_far_in,
    load_sem, near_send, near_recv, far_send, far_recv,
):
    i = lax.axis_index("stream")
    j = lax.axis_index("span")
    has = (i > 0, i < n_stream - 1, j > 0, j < n_span - 1)
    ids = ((i - 1, j), (i + 1, j), (i, j - 1), (i, j + 1))

    barrier = pltpu.get_barrier_semaphore()
    for side in range(4):
        @pl.when(has[side])
        def _():
            pl.semaphore_signal(barrier, inc=1, device_id=ids[side], device_id_type=MESH)

    load = pltpu.make_async_copy(q_hbm, wide.at[:, NEAR:NEAR + CX, PAD:PAD + CY, :], load_sem)
    load.start()

    for ref, width in ((wide, NEAR), (pre, FAR)):
        planes = CX + 2 * width

        @pl.when(~has[0])
        def _():
            ref[:, 0:width, :, :] = jnp.zeros((VARS, width, WY, CZ), F32)

        @pl.when(~has[1])
        def _():
            ref[:, width + CX:planes, :, :] = jnp.zeros((VARS, width, WY, CZ), F32)

        @pl.when(~has[2])
        def _():
            ref[:, width:width + CX, 0:PAD, :] = jnp.zeros((VARS, CX, PAD, CZ), F32)

        @pl.when(~has[3])
        def _():
            ref[:, width:width + CX, PAD + CY:WY, :] = jnp.zeros((VARS, CX, PAD, CZ), F32)

    load.wait()

    def column(ref, width, c, x, y):
        planes = CX + 2 * width
        flat = ref.reshape(VARS * planes * WY, CZ)
        return flat, pl.ds((c * planes + width + x) * WY + PAD + y, 8, WY)

    def pack(ref, out, width, side):
        for c in range(VARS):
            for m in range(width):
                for x in range(0, CX, 8):
                    flat, rows = column(ref, width, c, x, m if side == 2 else CY - width + m)
                    out[side - 2, c, m, x:x + 8, :] = flat[rows, :]

    def unpack(ref, held, width, side):
        for c in range(VARS):
            for m in range(width):
                for x in range(0, CX, 8):
                    flat, rows = column(ref, width, c, x, m - width if side == 2 else CY + m)
                    flat[rows, :] = held[side - 2, c, m, x:x + 8, :]

    def copy(ref, out, held, width, side, send, recv):
        if side == 0:
            src = ref.at[:, width:2 * width, PAD:PAD + CY, :]
            dst = ref.at[:, width + CX:2 * width + CX, PAD:PAD + CY, :]
        elif side == 1:
            src = ref.at[:, CX:width + CX, PAD:PAD + CY, :]
            dst = ref.at[:, 0:width, PAD:PAD + CY, :]
        else:
            src = out.at[side - 2]
            dst = held.at[3 - side]
        return pltpu.make_async_remote_copy(
            src_ref=src, dst_ref=dst, send_sem=send.at[side], recv_sem=recv.at[side ^ 1],
            device_id=ids[side], device_id_type=MESH,
        )

    def near(side):
        return copy(wide, y_near_out, y_near_in, NEAR, side, near_send, near_recv)

    def far(side):
        return copy(pre, y_far_out, y_far_in, FAR, side, far_send, far_recv)

    def start(make, side):
        @pl.when(has[side])
        def _():
            make(side).start()

    def finish_recv(make, side):
        @pl.when(has[side])
        def _():
            make(side ^ 1).wait_recv()

    def finish_send(make, side):
        @pl.when(has[side])
        def _():
            make(side).wait_send()

    expected = sum(jnp.where(flag, 1, 0) for flag in has)
    pl.semaphore_wait(barrier, expected)
    start(near, 0)
    start(near, 1)
    for side in (2, 3):
        pack(wide, y_near_out, NEAR, side)
        start(near, side)

    slope = band(((1, 8.0), (-1, -8.0), (2, -1.0), (-2, 1.0)))

    def base_plane(x, carry):
        q = wide[:, NEAR + x, PAD:PAD + CY, :]
        dz = along_z(q.reshape(VARS * CY, CZ), slope).reshape(VARS, CY, CZ) * (-1.0 / 36.0)
        for v in range(VARS):
            total = (4.0 * q[v] - old_ref[v, x]) * (1.0 / 3.0)
            for w in range(VARS):
                total = total + jac[50 + 5 * v + w] * dz[w]
            pre[v, FAR + x, PAD:PAD + CY, :] = total
        return carry

    lax.fori_loop(0, CX, base_plane, 0)

    for side in range(4):
        finish_recv(near, side)

    for side in (2, 3):
        @pl.when(has[side])
        def _():
            unpack(wide, y_near_in, NEAR, side)

    def rate_plane(x, carry):
        for tile in range(CY // 8):
            y = PAD + 8 * tile
            dx, dy = [], []
            for w in range(VARS):
                def at(sx, sy):
                    return wide[w, NEAR + x + sx, y + sy:y + sy + 8, :]

                dx.append((at(1, 0) - at(-1, 0)) * (-8.0 / 36.0) + (at(2, 0) - at(-2, 0)) * (1.0 / 36.0))
                dy.append((at(0, 1) - at(0, -1)) * (-8.0 / 36.0) + (at(0, 2) - at(0, -2)) * (1.0 / 36.0))
            for v in range(VARS):
                total = pre[v, FAR + x, y:y + 8, :]
                for w in range(VARS):
                    total = total + jac[5 * v + w] * dx[w]
                    total = total + jac[25 + 5 * v + w] * dy[w]
                pre[v, FAR + x, y:y + 8, :] = total
        return carry

    lax.fori_loop(0, FAR, rate_plane, 0)
    start(far, 0)
    lax.fori_loop(CX - FAR, CX, rate_plane, 0)
    start(far, 1)
    lax.fori_loop(FAR, CX - FAR, rate_plane, 0)
    for side in (2, 3):
        pack(pre, y_far_out, FAR, side)
        start(far, side)

    tenth = band(tuple((o, TAPS[abs(o)]) for o in range(-5, 6)))

    def filter_y(x, c, tile):
        y = PAD + 8 * tile

        def at(sy):
            return pre[c, FAR + x, y + sy:y + sy + 8, :]

        total = (TAPS[0] * SCALE) * at(0)
        for m in range(1, 6):
            total = total + (TAPS[m] * SCALE) * (at(m) + at(-m))
        return total

    def first_plane(x, carry):
        p = pre[:, FAR + x, PAD:PAD + CY, :]
        fz = along_z(p.reshape(VARS * CY, CZ), tenth).reshape(VARS, CY, CZ)
        total = p + SCALE * fz
        for c in range(VARS):
            for tile in range(CY // 8):
                part = total[c, 8 * tile:8 * tile + 8]
                if tile in (1, 2):
                    part = part + filter_y(x, c, tile)
                out_ref[c, x, 8 * tile:8 * tile + 8, :] = part
        return carry

    lax.fori_loop(0, CX, first_plane, 0)

    def filter_x(x, carry):
        for c in range(VARS):
            for tile in range(CY // 8):
                y = PAD + 8 * tile

                def at(sx):
                    return pre[c, FAR + x + sx, y:y + 8, :]

                total = out_ref[c, x, 8 * tile:8 * tile + 8, :] + (TAPS[0] * SCALE) * at(0)
                for m in range(1, 6):
                    total = total + (TAPS[m] * SCALE) * (at(m) + at(-m))
                out_ref[c, x, 8 * tile:8 * tile + 8, :] = total
        return carry

    lax.fori_loop(FAR, CX - FAR, filter_x, 0)
    for side in (0, 1):
        finish_recv(far, side)
    lax.fori_loop(0, FAR, filter_x, 0)
    lax.fori_loop(CX - FAR, CX, filter_x, 0)
    for side in (2, 3):
        finish_recv(far, side)

        @pl.when(has[side])
        def _():
            unpack(pre, y_far_in, FAR, side)

    def edge_plane(x, carry):
        for c in range(VARS):
            for tile in (0, CY // 8 - 1):
                rows = pl.ds(8 * tile, 8)
                out_ref[c, x, rows, :] = out_ref[c, x, rows, :] + filter_y(x, c, tile)
        return carry

    lax.fori_loop(0, CX, edge_plane, 0)
    for side in range(4):
        finish_send(near, side)
        finish_send(far, side)


def per_device(n_stream, n_span, q_now, q_prev, jacobians, fractions, send_blocks, recv_blocks):
    vmem = pl.BlockSpec(memory_space=pltpu.VMEM)
    anywhere = pl.BlockSpec(memory_space=pl.ANY)
    slots = GROUPS * n_span + 1
    width = n_span * SLOT
    sending = send_blocks.reshape(n_stream, 1, width)
    receiving = recv_blocks.reshape(n_stream, 1, width)
    offsets = fractions.reshape(3, n_stream, width)
    limit = 48 * 1024 * 1024
    packed, leaving = pl.pallas_call(
        functools.partial(pack_kernel, n_stream, n_span),
        name="pack",
        out_shape=(
            jax.ShapeDtypeStruct((ROWS, CZ), F32),
            jax.ShapeDtypeStruct((slots, ROW, 128), F32),
        ),
        in_specs=[anywhere, vmem, vmem],
        out_specs=(vmem, vmem),
        scratch_shapes=[
            pltpu.SMEM((GROUPS + 1, 1, width), jnp.int32),
            pltpu.SemaphoreType.DMA((2,)),
        ],
        compiler_params=pltpu.CompilerParams(vmem_limit_bytes=limit),
    )(sending, q_now, q_prev)
    fresh = pl.pallas_call(
        functools.partial(exchange_kernel, n_stream, n_span),
        name="exchange",
        out_shape=jax.ShapeDtypeStruct((slots, BRICK, 128), F32),
        in_specs=[vmem, vmem],
        out_specs=vmem,
        scratch_shapes=[
            pltpu.VMEM((slots, ROW, 128), F32),
            pltpu.SemaphoreType.DMA((slots,)),
            pltpu.SemaphoreType.DMA((slots,)),
        ],
        compiler_params=pltpu.CompilerParams(
            collective_id=0, has_side_effects=True, vmem_limit_bytes=limit
        ),
    )(offsets, leaving)
    shape = jax.ShapeDtypeStruct(q_now.shape, F32)
    now, older = pl.pallas_call(
        functools.partial(place_kernel, n_stream, n_span),
        name="place",
        out_shape=(shape, shape),
        in_specs=[anywhere, anywhere, vmem],
        out_specs=(vmem, vmem),
        scratch_shapes=[
            pltpu.SMEM((GROUPS + 1, 1, width), jnp.int32),
            pltpu.VMEM((ROWS, CZ), F32),
            pltpu.SemaphoreType.DMA((3,)),
        ],
        compiler_params=pltpu.CompilerParams(vmem_limit_bytes=limit),
    )(receiving, packed, fresh)
    return pl.pallas_call(
        functools.partial(advance_kernel, n_stream, n_span),
        name="advance",
        out_shape=shape,
        in_specs=[pl.BlockSpec(memory_space=pltpu.SMEM), anywhere, vmem],
        out_specs=vmem,
        scratch_shapes=[
            pltpu.VMEM((VARS, CX + 2 * NEAR, WY, CZ), F32),
            pltpu.VMEM((VARS, CX + 2 * FAR, WY, CZ), F32),
            pltpu.VMEM((2, VARS, NEAR, CX, CZ), F32),
            pltpu.VMEM((2, VARS, NEAR, CX, CZ), F32),
            pltpu.VMEM((2, VARS, FAR, CX, CZ), F32),
            pltpu.VMEM((2, VARS, FAR, CX, CZ), F32),
            pltpu.SemaphoreType.DMA,
            pltpu.SemaphoreType.DMA((4,)),
            pltpu.SemaphoreType.DMA((4,)),
            pltpu.SemaphoreType.DMA((4,)),
            pltpu.SemaphoreType.DMA((4,)),
        ],
        compiler_params=pltpu.CompilerParams(
            collective_id=1, has_side_effects=True, vmem_limit_bytes=limit
        ),
    )(jacobians.reshape(-1), now, older)


def solution(mesh):
    in_specs = (
        P(None, "stream", "span", None),
        P(None, "stream", "span", None),
        P(),
        P(None, ("stream", "span"), None),
        P(("stream", "span"), None),
        P(("stream", "span"), None),
    )
    out_specs = P(None, "stream", "span", None)
    body = functools.partial(per_device, mesh.shape["stream"], mesh.shape["span"])
    return jax.shard_map(
        body, mesh=mesh, in_specs=in_specs, out_specs=out_specs, check_vma=False
    )
```

profile of v0, /device:TPU:7, one launch (start us, length us, event | category | flops | bytes accessed | tf_op | source)
XLA Modules:
  0.0 55.7 jit_solution(4870793584108257009)
XLA Ops:
  0.0 0.0 copy-start
  0.0 1.3 %copy-done = f32[5,16,32,128]{3,2,1,0:T(8,128)S(1)} copy-done((f32[5,16,32,128]{3,2,1,0:T(8,128)S(1)}, f32[5,16,32,128]{3,2,1,0:T(8,128)}, u32[]{:S(2)}) %copy-start) | copy-done | bytes 1310744
  1.3 0.0 copy-start.1
  1.3 1.3 %copy-done.1 = f32[5,16,32,128]{3,2,1,0:T(8,128)S(1)} copy-done((f32[5,16,32,128]{3,2,1,0:T(8,128)S(1)}, f32[5,16,32,128]{3,2,1,0:T(8,128)}, u32[]{:S(2)}) %copy-start.1) | copy-done | bytes 1310744
  2.6 0.0 copy-start.3
  2.6 0.7 %copy-done.3 = s32[1,4096]{1,0:T(1,128)S(1)} copy-done((s32[1,4096]{1,0:T(1,128)S(1)}, s32[1,4096]{1,0:T(1,128)}, u32[]{:S(2)}) %copy-start.3) | copy-done | bytes 16408
  3.4 0.0 copy-start.2
  3.4 0.0 copy-start.4
  3.4 6.7 %pack.1 = (f32[5120,128]{1,0:T(8,128)S(1)}, f32[21,20,128]{2,1,0:T(8,128)S(1)}) custom-call(s32[32,1,128]{2,1,0:T(1,128)S(1)} %bitcast.4, f32[5,16,32,128]{3,2,1,0:T(8,128)S(1)} %copy-done, f32[5,16,32,128]{3,2,1,0:T(8,128)S(1)} %copy-done.1), custom_call_target="tpu_custom_call" | custom-call | tf_op jit(solution)/shard_map/pack/pallas_call | solution.py:489
  10.0 0.0 copy-done.2
  10.0 14.4 %exchange.1.fresh_ref = f32[21,40,128]{2,1,0:T(8,128)S(1)} custom-call(f32[3,32,128]{2,1,0:T(8,128)S(1)} %bitcast.3, f32[21,20,128]{2,1,0:T(8,128)S(1)} %get-tuple-element.10.sending), custom_call_target="tpu_custom_call" | custom-call | tf_op jit(solution)/shard_map/exchange/pallas_call | solution.py:504
  24.5 0.0 copy-done.4
  24.5 0.0 copy-start.5
  24.5 9.0 %place.1 = (f32[5,16,32,128]{3,2,1,0:T(8,128)S(1)}, f32[5,16,32,128]{3,2,1,0:T(8,128)S(1)}) custom-call(s32[32,1,128]{2,1,0:T(1,128)S(1)} %bitcast.5, f32[5120,128]{1,0:T(8,128)S(1)} %get-tuple-element.9.packed_hbm, f32[21,40,128]{2,1,0:T(8,128)S(1)} %exchange.1.fresh_ref), custom_call_target="tpu_custom_call" | custom-call | tf_op jit(solution)/shard_map/place/pallas_call | solution.py:520
  33.5 0.0 copy-done.5
  33.5 0.1 reshape.12.jac
  33.6 21.0 %advance.1 = f32[5,16,32,128]{3,2,1,0:T(8,128)S(1)} custom-call(f32[75]{0:T(128)S(1)} %reshape.12.jac, f32[5,16,32,128]{3,2,1,0:T(8,128)S(1)} %get-tuple-element.11.q_hbm, f32[5,16,32,128]{3,2,1,0:T(8,128)S(1)} %get-tuple-element.12.old_ref), custom_call_target="tpu_custom_call" | custom-call | tf_op jit(solution)/shard_map/advance/pallas_call | solution.py:533
  54.6 1.1 %copy.10 = f32[5,16,32,128]{3,2,1,0:T(8,128)} copy(f32[5,16,32,128]{3,2,1,0:T(8,128)S(1)} %advance.1) | data formatting | bytes 2621440
  (1 shorter events, 0.0 us)
Async XLA Ops:
  0.0 1.3 %copy-start = (f32[5,16,32,128]{3,2,1,0:T(8,128)S(1)}, f32[5,16,32,128]{3,2,1,0:T(8,128)}, u32[]{:S(2)}) copy-start(f32[5,16,32,128]{3,2,1,0:T(8,128)} %now_ref.1) | copy-start | bytes 3932164
  1.3 1.3 %copy-start.1 = (f32[5,16,32,128]{3,2,1,0:T(8,128)S(1)}, f32[5,16,32,128]{3,2,1,0:T(8,128)}, u32[]{:S(2)}) copy-start(f32[5,16,32,128]{3,2,1,0:T(8,128)} %prev_ref.1) | copy-start | bytes 3932164
  2.6 0.7 %copy-start.3 = (s32[1,4096]{1,0:T(1,128)S(1)}, s32[1,4096]{1,0:T(1,128)}, u32[]{:S(2)}) copy-start(s32[1,4096]{1,0:T(1,128)} %param.10) | copy-start | bytes 49156
  3.4 6.7 %copy-start.2 = (f32[3,1,4096]{2,1,0:T(1,128)S(1)}, f32[3,1,4096]{2,1,0:T(1,128)}, u32[]{:S(2)}) copy-start(f32[3,1,4096]{2,1,0:T(1,128)} %param.9) | copy-start | bytes 147460
  3.4 21.1 %copy-start.4 = (s32[1,4096]{1,0:T(1,128)S(1)}, s32[1,4096]{1,0:T(1,128)}, u32[]{:S(2)}) copy-start(s32[1,4096]{1,0:T(1,128)} %param.11) | copy-start | bytes 49156
  24.5 9.0 %copy-start.5 = (f32[3,5,5]{2,0,1:T(4,128)S(1)}, f32[3,5,5]{2,0,1:T(4,128)}, u32[]{:S(2)}) copy-start(f32[3,5,5]{2,0,1:T(4,128)} %param.8) | copy-start | bytes 904
where the time goes:
time: 55.9 us; the launch traced here: 55.7 us
  Pallas kernels  51.1 us (91%)
  local copies, waits for them, and re-layouts  4.51 us (8%)
    pallas_call x1, Pallas kernels, per_device(): pl.pallas_call(functools.partial(advance_kernel, n_stream, n_span), name=...  21 us
    pallas_call x1, Pallas kernels, per_device(): pl.pallas_call(functools.partial(exchange_kernel, n_stream, n_span), name...  14.4 us
    pallas_call x1, Pallas kernels, per_device(): pl.pallas_call(functools.partial(place_kernel, n_stream, n_span), name='p...  8.99 us
    pallas_call x1, Pallas kernels, per_device(): pl.pallas_call(functools.partial(pack_kernel, n_stream, n_span), name='pa...  6.66 us
    unnamed x14, local copies, waits for them, and re-layouts  4.42 us

commit v1 on v0

--- a/solution.py
+++ b/solution.py
@@ -34,18 +34,37 @@
     return jnp.minimum(jnp.maximum(i - REACH, 0), n_stream - GROUPS)
 
 
-def pack_kernel(n_stream, n_span, send_hbm, now_ref, prev_ref, packed_ref, sending_ref, picks, sem):
+def exchange_kernel(
+    n_stream, n_span, send_hbm, frac_ref, now_ref, prev_ref, packed_ref, fresh_ref,
+    picks, sending, arrived, pick_sem, send_sem, recv_sem,
+):
     i = lax.axis_index("stream")
     j = lax.axis_index("span")
     first = window_start(i, n_stream)
     far = lax.rem(i + n_stream // 2, n_stream)
     near_count = GROUPS * n_span
-    copies = [
-        pltpu.make_async_copy(send_hbm.at[pl.ds(first, GROUPS)], picks.at[pl.ds(0, GROUPS)], sem.at[0]),
-        pltpu.make_async_copy(send_hbm.at[pl.ds(far, 1)], picks.at[pl.ds(GROUPS, 1)], sem.at[1]),
-    ]
-    for copy in copies:
-        copy.start()
+    far_slot = near_count
+
+    def is_partner(g, jp):
+        t = first + g
+        return (t >= i - REACH) & (t <= i + REACH) & ((t != i) | (jp != j))
+
+    barrier = pltpu.get_barrier_semaphore()
+    for g in range(GROUPS):
+        for jp in range(n_span):
+            @pl.when(is_partner(g, jp))
+            def _():
+                pl.semaphore_signal(barrier, inc=1, device_id=(first + g, jp), device_id_type=MESH)
+    pl.semaphore_signal(barrier, inc=1, device_id=(far, j), device_id_type=MESH)
+
+    near_picks = pltpu.make_async_copy(
+        send_hbm.at[pl.ds(first, GROUPS)], picks.at[pl.ds(0, GROUPS)], pick_sem.at[0]
+    )
+    far_picks = pltpu.make_async_copy(
+        send_hbm.at[pl.ds(far, 1)], picks.at[pl.ds(GROUPS, 1)], pick_sem.at[1]
+    )
+    near_picks.start()
+    far_picks.start()
 
     def relayout(xb, carry):
         for dx in range(2):
@@ -57,62 +76,30 @@
         return carry
 
     lax.fori_loop(0, BX, relayout, 0)
-    for copy in copies:
-        copy.wait()
+    near_picks.wait()
+    far_picks.wait()
+
+    rows_near = jnp.minimum(i + REACH, n_stream - 1) - jnp.maximum(i - REACH, 0) + 1
+    pl.semaphore_wait(barrier, rows_near * n_span)
+
     half = lanes((ROW, 128)) < 64
     pair = lanes((BRICK, 128)) // 2
-    chunk = 8
-
-    def pack(p, carry):
-        row = p // n_span
-        start = jnp.where(p < near_count, lax.rem(p, n_span), j) * SLOT
-
-        def some(head, total):
-            def more(total):
-                for k in range(head, head + chunk):
-                    brick = jnp.maximum(picks[row, 0, start + k], 0)
-                    base = pl.multiple_of((brick >> 6) * BRICK, 8)
-                    shift = (2 * k - 2 * (brick & 63)) & 127
-                    moved = pltpu.roll(packed_ref[pl.ds(base, BRICK), :], shift, 1)
-                    total = jnp.where(pair == k, moved, total)
-                return total
-            return lax.cond(picks[row, 0, start + head] >= 0, more, lambda total: total, total)
-
+
+    def pack(row, start):
         total = jnp.zeros((BRICK, 128), F32)
-        for head in range(0, SLOT, chunk):
-            total = some(head, total)
-        sending_ref[p] = jnp.where(half, total[:ROW], pltpu.roll(total[ROW:], 64, 1))
-        return carry
-
-    lax.fori_loop(0, near_count + 1, pack, 0)
-
-
-def exchange_kernel(n_stream, n_span, frac_ref, sending, fresh_ref, arrived, send_sem, recv_sem):
-    i = lax.axis_index("stream")
-    j = lax.axis_index("span")
-    first = window_start(i, n_stream)
-    far = lax.rem(i + n_stream // 2, n_stream)
-    near_count = GROUPS * n_span
-    far_slot = near_count
-
-    def is_partner(g, jp):
-        t = first + g
-        return (t >= i - REACH) & (t <= i + REACH) & ((t != i) | (jp != j))
-
-    barrier = pltpu.get_barrier_semaphore()
-    for g in range(GROUPS):
-        for jp in range(n_span):
-            @pl.when(is_partner(g, jp))
-            def _():
-                pl.semaphore_signal(barrier, inc=1, device_id=(first + g, jp), device_id_type=MESH)
-    pl.semaphore_signal(barrier, inc=1, device_id=(far, j), device_id_type=MESH)
-
-    rows_near = jnp.minimum(i + REACH, n_stream - 1) - jnp.maximum(i - REACH, 0) + 1
-    pl.semaphore_wait(barrier, rows_near * n_span)
+        for k in range(SLOT):
+            brick = jnp.maximum(picks[row, 0, start + k], 0)
+            base = (brick >> 6) * BRICK
+            moved = pltpu.roll(packed_ref[pl.ds(base, BRICK), :], (2 * k - 2 * (brick & 63)) & 127, 1)
+            total = jnp.where(pair == k, moved, total)
+        return jnp.where(half, total[:ROW], pltpu.roll(total[ROW:], 64, 1))
+
+    my_far_slot = far_slot
+    sending[far_slot] = pack(GROUPS, j * SLOT)
 
     def far_copy():
         return pltpu.make_async_remote_copy(
-            src_ref=sending.at[far_slot], dst_ref=arrived.at[far_slot],
+            src_ref=sending.at[far_slot], dst_ref=arrived.at[my_far_slot],
             send_sem=send_sem.at[far_slot], recv_sem=recv_sem.at[far_slot],
             device_id=(far, j), device_id_type=MESH,
         )
@@ -142,6 +129,10 @@
         g = p // n_span
         jp = lax.rem(p, n_span)
         t = first + g
+
+        @pl.when((t >= i - REACH) & (t <= i + REACH))
+        def _():
+            sending[p] = pack(g, jp * SLOT)
 
         @pl.when(is_partner(g, jp))
         def _():
@@ -486,36 +477,27 @@
     receiving = recv_blocks.reshape(n_stream, 1, width)
     offsets = fractions.reshape(3, n_stream, width)
     limit = 48 * 1024 * 1024
-    packed, leaving = pl.pallas_call(
-        functools.partial(pack_kernel, n_stream, n_span),
-        name="pack",
+    packed, fresh = pl.pallas_call(
+        functools.partial(exchange_kernel, n_stream, n_span),
+        name="exchange",
         out_shape=(
             jax.ShapeDtypeStruct((ROWS, CZ), F32),
-            jax.ShapeDtypeStruct((slots, ROW, 128), F32),
+            jax.ShapeDtypeStruct((slots, BRICK, 128), F32),
         ),
-        in_specs=[anywhere, vmem, vmem],
+        in_specs=[anywhere, vmem, vmem, vmem],
         out_specs=(vmem, vmem),
         scratch_shapes=[
             pltpu.SMEM((GROUPS + 1, 1, width), jnp.int32),
+            pltpu.VMEM((slots, ROW, 128), F32),
+            pltpu.VMEM((slots, ROW, 128), F32),
             pltpu.SemaphoreType.DMA((2,)),
-        ],
-        compiler_params=pltpu.CompilerParams(vmem_limit_bytes=limit),
-    )(sending, q_now, q_prev)
-    fresh = pl.pallas_call(
-        functools.partial(exchange_kernel, n_stream, n_span),
-        name="exchange",
-        out_shape=jax.ShapeDtypeStruct((slots, BRICK, 128), F32),
-        in_specs=[vmem, vmem],
-        out_specs=vmem,
-        scratch_shapes=[
-            pltpu.VMEM((slots, ROW, 128), F32),
             pltpu.SemaphoreType.DMA((slots,)),
             pltpu.SemaphoreType.DMA((slots,)),
         ],
         compiler_params=pltpu.CompilerParams(
             collective_id=0, has_side_effects=True, vmem_limit_bytes=limit
         ),
-    )(offsets, leaving)
+    )(sending, offsets, q_now, q_prev)
     shape = jax.ShapeDtypeStruct(q_now.shape, F32)
     now, older = pl.pallas_call(
         functools.partial(place_kernel, n_stream, n_span),

time: 55.9 us -> 52.4 us (0.937)
  the two profiles are of different devices: /device:TPU:7 before, /device:TPU:104 now
where the time goes in v1:
time: 52.4 us; the launch traced here: 52.1 us
  Pallas kernels  46.8 us (89%)
  local copies, waits for them, and re-layouts  5.3 us (10%)
    pallas_call x1, Pallas kernels, per_device(): pl.pallas_call(functools.partial(exchange_kernel, n_stream, n_span), name...  18.8 us
    pallas_call x1, Pallas kernels, per_device(): pl.pallas_call(functools.partial(advance_kernel, n_stream, n_span), name=...  18.1 us
    pallas_call x1, Pallas kernels, per_device(): pl.pallas_call(functools.partial(place_kernel, n_stream, n_span), name='p...  9.86 us
    unnamed x14, local copies, waits for them, and re-layouts  5.22 us

profile of v1, /device:TPU:104, one launch (start us, length us, event | category | flops | bytes accessed | tf_op | source)
XLA Modules:
  0.0 52.1 jit_solution(10402653610781467295)
XLA Ops:
  0.0 0.0 copy-start
  0.0 1.3 %copy-done = f32[5,16,32,128]{3,2,1,0:T(8,128)S(1)} copy-done((f32[5,16,32,128]{3,2,1,0:T(8,128)S(1)}, f32[5,16,32,128]{3,2,1,0:T(8,128)}, u32[]{:S(2)}) %copy-start) | copy-done | bytes 1310744
  1.3 0.0 copy-start.1
  1.3 1.3 %copy-done.1 = f32[5,16,32,128]{3,2,1,0:T(8,128)S(1)} copy-done((f32[5,16,32,128]{3,2,1,0:T(8,128)S(1)}, f32[5,16,32,128]{3,2,1,0:T(8,128)}, u32[]{:S(2)}) %copy-start.1) | copy-done | bytes 1310744
  2.6 0.0 copy-start.2
  2.6 0.8 %copy-done.2 = f32[3,1,4096]{2,1,0:T(1,128)S(1)} copy-done((f32[3,1,4096]{2,1,0:T(1,128)S(1)}, f32[3,1,4096]{2,1,0:T(1,128)}, u32[]{:S(2)}) %copy-start.2) | copy-done | bytes 49176
  3.4 0.0 copy-start.3
  3.4 0.7 %copy-done.3 = s32[1,4096]{1,0:T(1,128)S(1)} copy-done((s32[1,4096]{1,0:T(1,128)S(1)}, s32[1,4096]{1,0:T(1,128)}, u32[]{:S(2)}) %copy-start.3) | copy-done | bytes 16408
  4.2 0.0 copy-start.4
  4.2 18.8 %exchange.1 = (f32[5120,128]{1,0:T(8,128)S(1)}, f32[21,40,128]{2,1,0:T(8,128)S(1)}) custom-call(s32[32,1,128]{2,1,0:T(1,128)S(1)} %bitcast.4, f32[3,32,128]{2,1,0:T(8,128)S(1)} %bitcast.3, f32[5,16,32,128]{3,2,1,0:T(8,128)S(1)} %copy-done, f32[5,16,32,128]{3,2,1,0:T(8,128)S(1)} %copy-done.1), custom_call_target="tpu_custom_call" | custom-call | tf_op jit(solution)/shard_map/exchange/pallas_call | solution.py:480
  23.0 0.0 copy-done.4
  23.0 0.0 copy-start.5
  23.0 9.9 %place.1 = (f32[5,16,32,128]{3,2,1,0:T(8,128)S(1)}, f32[5,16,32,128]{3,2,1,0:T(8,128)S(1)}) custom-call(s32[32,1,128]{2,1,0:T(1,128)S(1)} %bitcast.5, f32[5120,128]{1,0:T(8,128)S(1)} %get-tuple-element.9.packed_hbm, f32[21,40,128]{2,1,0:T(8,128)S(1)} %get-tuple-element.10.fresh_ref), custom_call_target="tpu_custom_call" | custom-call | tf_op jit(solution)/shard_map/place/pallas_call | solution.py:502
  32.9 0.0 copy-done.5
  32.9 0.1 reshape.12.jac
  33.0 18.1 %advance.1 = f32[5,16,32,128]{3,2,1,0:T(8,128)S(1)} custom-call(f32[75]{0:T(128)S(1)} %reshape.12.jac, f32[5,16,32,128]{3,2,1,0:T(8,128)S(1)} %get-tuple-element.11.q_hbm, f32[5,16,32,128]{3,2,1,0:T(8,128)S(1)} %get-tuple-element.12.old_ref), custom_call_target="tpu_custom_call" | custom-call | tf_op jit(solution)/shard_map/advance/pallas_call | solution.py:515
  51.1 1.1 %copy.10 = f32[5,16,32,128]{3,2,1,0:T(8,128)} copy(f32[5,16,32,128]{3,2,1,0:T(8,128)S(1)} %advance.1) | data formatting | bytes 2621440
  (1 shorter events, 0.0 us)
Async XLA Ops:
  0.0 1.3 %copy-start = (f32[5,16,32,128]{3,2,1,0:T(8,128)S(1)}, f32[5,16,32,128]{3,2,1,0:T(8,128)}, u32[]{:S(2)}) copy-start(f32[5,16,32,128]{3,2,1,0:T(8,128)} %now_ref.1) | copy-start | bytes 3932164
  1.3 1.3 %copy-start.1 = (f32[5,16,32,128]{3,2,1,0:T(8,128)S(1)}, f32[5,16,32,128]{3,2,1,0:T(8,128)}, u32[]{:S(2)}) copy-start(f32[5,16,32,128]{3,2,1,0:T(8,128)} %prev_ref.1) | copy-start | bytes 3932164
  2.6 0.8 %copy-start.2 = (f32[3,1,4096]{2,1,0:T(1,128)S(1)}, f32[3,1,4096]{2,1,0:T(1,128)}, u32[]{:S(2)}) copy-start(f32[3,1,4096]{2,1,0:T(1,128)} %param.9) | copy-start | bytes 147460
  3.4 0.7 %copy-start.3 = (s32[1,4096]{1,0:T(1,128)S(1)}, s32[1,4096]{1,0:T(1,128)}, u32[]{:S(2)}) copy-start(s32[1,4096]{1,0:T(1,128)} %param.10) | copy-start | bytes 49156
  4.2 18.8 %copy-start.4 = (s32[1,4096]{1,0:T(1,128)S(1)}, s32[1,4096]{1,0:T(1,128)}, u32[]{:S(2)}) copy-start(s32[1,4096]{1,0:T(1,128)} %param.11) | copy-start | bytes 49156
  23.0 9.9 %copy-start.5 = (f32[3,5,5]{2,0,1:T(4,128)S(1)}, f32[3,5,5]{2,0,1:T(4,128)}, u32[]{:S(2)}) copy-start(f32[3,5,5]{2,0,1:T(4,128)} %param.8) | copy-start | bytes 904

commit v2 on v1

--- a/solution.py
+++ b/solution.py
@@ -85,30 +85,24 @@
     half = lanes((ROW, 128)) < 64
     pair = lanes((BRICK, 128)) // 2
 
-    def pack(row, start):
+    def pack(p, row, start):
         total = jnp.zeros((BRICK, 128), F32)
         for k in range(SLOT):
             brick = jnp.maximum(picks[row, 0, start + k], 0)
-            base = (brick >> 6) * BRICK
-            moved = pltpu.roll(packed_ref[pl.ds(base, BRICK), :], (2 * k - 2 * (brick & 63)) & 127, 1)
+            moved = pltpu.roll(
+                packed_ref[pl.ds((brick >> 6) * BRICK, BRICK), :], (2 * k - 2 * (brick & 63)) & 127, 1
+            )
             total = jnp.where(pair == k, moved, total)
-        return jnp.where(half, total[:ROW], pltpu.roll(total[ROW:], 64, 1))
-
-    my_far_slot = far_slot
-    sending[far_slot] = pack(GROUPS, j * SLOT)
+        sending[p] = jnp.where(half, total[:ROW], pltpu.roll(total[ROW:], 64, 1))
 
     def far_copy():
         return pltpu.make_async_remote_copy(
-            src_ref=sending.at[far_slot], dst_ref=arrived.at[my_far_slot],
+            src_ref=sending.at[far_slot], dst_ref=arrived.at[far_slot],
             send_sem=send_sem.at[far_slot], recv_sem=recv_sem.at[far_slot],
             device_id=(far, j), device_id_type=MESH,
         )
 
-    far_copy().start()
-
-    def near_copy(p):
-        g = p // n_span
-        jp = lax.rem(p, n_span)
+    def near_copy(p, g, jp):
         t = first + g
         slot = (i - window_start(t, n_stream)) * n_span + j
         slot = jnp.minimum(jnp.maximum(slot, 0), near_count - 1)
@@ -122,25 +116,29 @@
         return pltpu.make_async_remote_copy(
             src_ref=sending.at[p], dst_ref=arrived.at[p],
             send_sem=send_sem.at[p], recv_sem=recv_sem.at[p],
-            device_id=(first + p // n_span, lax.rem(p, n_span)), device_id_type=MESH,
+            device_id=(first + p // n_span, p % n_span), device_id_type=MESH,
         )
 
-    def send(p, carry):
-        g = p // n_span
-        jp = lax.rem(p, n_span)
+    pack(far_slot, GROUPS, j * SLOT)
+    far_copy().start()
+
+    def send(n, carry):
+        turn = n // 2
+        g = jnp.where(n == 2 * turn, turn, GROUPS - 1 - turn)
         t = first + g
 
         @pl.when((t >= i - REACH) & (t <= i + REACH))
         def _():
-            sending[p] = pack(g, jp * SLOT)
-
-        @pl.when(is_partner(g, jp))
-        def _():
-            near_copy(p).start()
-
-        return carry
-
-    lax.fori_loop(0, near_count, send, 0)
+            for jp in range(n_span):
+                pack(g * n_span + jp, g, jp * SLOT)
+            for jp in range(n_span):
+                @pl.when((t != i) | (jp != j))
+                def _():
+                    near_copy(g * n_span + jp, g, jp).start()
+
+        return carry
+
+    lax.fori_loop(0, GROUPS, send, 0)
     own = (i - first) * n_span + j
     arrived[own] = sending[own]
 
@@ -173,15 +171,21 @@
         fresh_ref[p, ROW:BRICK, :] = pltpu.roll(both, 64, 1)
 
     for p in range(near_count):
+        @pl.when(is_partner(p // n_span, p % n_span))
+        def _():
+            arrival(p).wait_recv()
+
+    far_copy().wait_recv()
+    for p in range(near_count):
         g, jp = p // n_span, p % n_span
-
-        @pl.when(is_partner(g, jp))
-        def _():
-            arrival(p).wait()
-
         finish(p, *(spreads[jp][6 * d + g:6 * d + g + 1] for d in range(3)))
-    far_copy().wait()
     finish(far_slot, *(far_spread[6 * d + GROUPS:6 * d + GROUPS + 1] for d in range(3)))
+    for p in range(near_count):
+        @pl.when(is_partner(p // n_span, p % n_span))
+        def _():
+            arrival(p).wait_send()
+
+    far_copy().wait_send()
 
 
 def place_kernel(n_stream, n_span, recv_hbm, packed_hbm, fresh_ref, now_ref, prev_ref, targets, work, sem):
@@ -200,27 +204,25 @@
     for copy in copies:
         copy.wait()
     pair = lanes((BRICK, 128)) // 2
-    chunk = 8
-
-    def put(p, carry):
-        row = p // n_span
-        start = jnp.where(p < near_count, lax.rem(p, n_span), j) * SLOT
-        for head in range(0, SLOT, chunk):
-            @pl.when(targets[row, 0, start + head] >= 0)
-            def _():
-                block = fresh_ref[p]
-                for k in range(head, head + chunk):
-                    target = targets[row, 0, start + k]
-                    brick = jnp.maximum(target, 0)
-                    column = lax.rem(brick, 64)
-                    base = pl.multiple_of((brick // 64) * BRICK, 8)
-                    shift = lax.rem(2 * column - 2 * k + 128, 128)
-                    moved = pltpu.roll(block, shift, 1)
-                    mark = jnp.where(target >= 0, column, -1)
-                    pltpu.store(work.at[pl.ds(base, BRICK), :], moved, mask=pair == mark)
-        return carry
-
-    lax.fori_loop(0, near_count + 1, put, 0)
+
+    def put(p, row, start):
+        block = fresh_ref[p]
+        for k in range(SLOT):
+            target = targets[row, 0, start + k]
+            brick = jnp.maximum(target, 0)
+            column = brick & 63
+            moved = pltpu.roll(block, (2 * column - 2 * k) & 127, 1)
+            mark = jnp.where(target >= 0, column, -1)
+            base = pl.multiple_of((brick >> 6) * BRICK, 8)
+            pltpu.store(work.at[pl.ds(base, BRICK), :], moved, mask=pair == mark)
+
+    def put_group(g, carry):
+        for jp in range(n_span):
+            put(g * n_span + jp, g, jp * SLOT)
+        return carry
+
+    lax.fori_loop(0, GROUPS, put_group, 0)
+    put(near_count, GROUPS, j * SLOT)
 
     def relayout(xb, carry):
         for dx in range(2):

time: 52.4 us -> 42.7 us (0.81)
  the two profiles are of different devices: /device:TPU:104 before, /device:TPU:7 now
where the time goes in v2:
time: 42.7 us; the launch traced here: 42.5 us
  Pallas kernels  37.1 us (87%)
  local copies, waits for them, and re-layouts  5.3 us (12%)
    pallas_call x1, Pallas kernels, per_device(): pl.pallas_call(functools.partial(advance_kernel, n_stream, n_span), name=...  17.8 us
    pallas_call x1, Pallas kernels, per_device(): pl.pallas_call(functools.partial(exchange_kernel, n_stream, n_span), name...  14.4 us
    unnamed x14, local copies, waits for them, and re-layouts  5.22 us
    pallas_call x1, Pallas kernels, per_device(): pl.pallas_call(functools.partial(place_kernel, n_stream, n_span), name='p...  4.85 us

profile of v2, /device:TPU:7, one launch (start us, length us, event | category | flops | bytes accessed | tf_op | source)
XLA Modules:
  0.0 42.5 jit_solution(5785776236674695239)
XLA Ops:
  0.0 0.0 copy-start
  0.0 1.3 %copy-done = f32[5,16,32,128]{3,2,1,0:T(8,128)S(1)} copy-done((f32[5,16,32,128]{3,2,1,0:T(8,128)S(1)}, f32[5,16,32,128]{3,2,1,0:T(8,128)}, u32[]{:S(2)}) %copy-start) | copy-done | bytes 1310744
  1.3 0.0 copy-start.1
  1.3 1.3 %copy-done.1 = f32[5,16,32,128]{3,2,1,0:T(8,128)S(1)} copy-done((f32[5,16,32,128]{3,2,1,0:T(8,128)S(1)}, f32[5,16,32,128]{3,2,1,0:T(8,128)}, u32[]{:S(2)}) %copy-start.1) | copy-done | bytes 1310744
  2.6 0.0 copy-start.2
  2.6 0.8 %copy-done.2 = f32[3,1,4096]{2,1,0:T(1,128)S(1)} copy-done((f32[3,1,4096]{2,1,0:T(1,128)S(1)}, f32[3,1,4096]{2,1,0:T(1,128)}, u32[]{:S(2)}) %copy-start.2) | copy-done | bytes 49176
  3.4 0.0 copy-start.3
  3.4 0.7 %copy-done.3 = s32[1,4096]{1,0:T(1,128)S(1)} copy-done((s32[1,4096]{1,0:T(1,128)S(1)}, s32[1,4096]{1,0:T(1,128)}, u32[]{:S(2)}) %copy-start.3) | copy-done | bytes 16408
  4.2 0.0 copy-start.4
  4.2 14.4 %exchange.1 = (f32[5120,128]{1,0:T(8,128)S(1)}, f32[21,40,128]{2,1,0:T(8,128)S(1)}) custom-call(s32[32,1,128]{2,1,0:T(1,128)S(1)} %bitcast.4, f32[3,32,128]{2,1,0:T(8,128)S(1)} %bitcast.3, f32[5,16,32,128]{3,2,1,0:T(8,128)S(1)} %copy-done, f32[5,16,32,128]{3,2,1,0:T(8,128)S(1)} %copy-done.1), custom_call_target="tpu_custom_call" | custom-call | tf_op jit(solution)/shard_map/exchange/pallas_call | solution.py:482
  18.6 0.0 copy-done.4
  18.6 0.0 copy-start.5
  18.6 4.8 %place.1 = (f32[5,16,32,128]{3,2,1,0:T(8,128)S(1)}, f32[5,16,32,128]{3,2,1,0:T(8,128)S(1)}) custom-call(s32[32,1,128]{2,1,0:T(1,128)S(1)} %bitcast.5, f32[5120,128]{1,0:T(8,128)S(1)} %get-tuple-element.9.packed_hbm, f32[21,40,128]{2,1,0:T(8,128)S(1)} %get-tuple-element.10.fresh_ref), custom_call_target="tpu_custom_call" | custom-call | tf_op jit(solution)/shard_map/place/pallas_call | solution.py:504
  23.5 0.0 copy-done.5
  23.5 0.1 reshape.12.jac
  23.6 17.8 %advance.1 = f32[5,16,32,128]{3,2,1,0:T(8,128)S(1)} custom-call(f32[75]{0:T(128)S(1)} %reshape.12.jac, f32[5,16,32,128]{3,2,1,0:T(8,128)S(1)} %get-tuple-element.11.q_hbm, f32[5,16,32,128]{3,2,1,0:T(8,128)S(1)} %get-tuple-element.12.old_ref), custom_call_target="tpu_custom_call" | custom-call | tf_op jit(solution)/shard_map/advance/pallas_call | solution.py:517
  41.4 1.1 %copy.10 = f32[5,16,32,128]{3,2,1,0:T(8,128)} copy(f32[5,16,32,128]{3,2,1,0:T(8,128)S(1)} %advance.1) | data formatting | bytes 2621440
  (1 shorter events, 0.0 us)
Async XLA Ops:
  0.0 1.3 %copy-start = (f32[5,16,32,128]{3,2,1,0:T(8,128)S(1)}, f32[5,16,32,128]{3,2,1,0:T(8,128)}, u32[]{:S(2)}) copy-start(f32[5,16,32,128]{3,2,1,0:T(8,128)} %now_ref.1) | copy-start | bytes 3932164
  1.3 1.3 %copy-start.1 = (f32[5,16,32,128]{3,2,1,0:T(8,128)S(1)}, f32[5,16,32,128]{3,2,1,0:T(8,128)}, u32[]{:S(2)}) copy-start(f32[5,16,32,128]{3,2,1,0:T(8,128)} %prev_ref.1) | copy-start | bytes 3932164
  2.6 0.8 %copy-start.2 = (f32[3,1,4096]{2,1,0:T(1,128)S(1)}, f32[3,1,4096]{2,1,0:T(1,128)}, u32[]{:S(2)}) copy-start(f32[3,1,4096]{2,1,0:T(1,128)} %param.9) | copy-start | bytes 147460
  3.4 0.7 %copy-start.3 = (s32[1,4096]{1,0:T(1,128)S(1)}, s32[1,4096]{1,0:T(1,128)}, u32[]{:S(2)}) copy-start(s32[1,4096]{1,0:T(1,128)} %param.10) | copy-start | bytes 49156
  4.2 14.4 %copy-start.4 = (s32[1,4096]{1,0:T(1,128)S(1)}, s32[1,4096]{1,0:T(1,128)}, u32[]{:S(2)}) copy-start(s32[1,4096]{1,0:T(1,128)} %param.11) | copy-start | bytes 49156
  18.6 4.9 %copy-start.5 = (f32[3,5,5]{2,0,1:T(4,128)S(1)}, f32[3,5,5]{2,0,1:T(4,128)}, u32[]{:S(2)}) copy-start(f32[3,5,5]{2,0,1:T(4,128)} %param.8) | copy-start | bytes 904

commit v3 on v2

--- a/solution.py
+++ b/solution.py
@@ -13,6 +13,8 @@
 CHANS = 10
 SLOT = 32
 REACH = 2
+PARTS = 4
+EARLY = 2
 GROUPS = 2 * REACH + 1
 CX, CY, CZ = 16, 32, 128
 BX, BY = CX // 2, CY // 2
@@ -35,8 +37,8 @@
 
 
 def exchange_kernel(
-    n_stream, n_span, send_hbm, frac_ref, now_ref, prev_ref, packed_ref, fresh_ref,
-    picks, sending, arrived, pick_sem, send_sem, recv_sem,
+    n_stream, n_span, send_hbm, frac_hbm, now_hbm, prev_hbm, packed_ref, fresh_ref,
+    picks, frac_ref, now_ref, prev_ref, sending, arrived, pick_sem, load_sem, send_sem, recv_sem,
 ):
     i = lax.axis_index("stream")
     j = lax.axis_index("span")
@@ -49,6 +51,27 @@
         t = first + g
         return (t >= i - REACH) & (t <= i + REACH) & ((t != i) | (jp != j))
 
+    loads = [
+        pltpu.make_async_copy(
+            src.at[:, pl.ds(part * CX // PARTS, CX // PARTS)],
+            dst.at[:, pl.ds(part * CX // PARTS, CX // PARTS)],
+            load_sem.at[2 * part + n],
+        )
+        for part in range(PARTS)
+        for n, (src, dst) in enumerate(((now_hbm, now_ref), (prev_hbm, prev_ref)))
+    ]
+    others = [
+        pltpu.make_async_copy(
+            send_hbm.at[pl.ds(first, GROUPS)], picks.at[pl.ds(0, GROUPS)], pick_sem.at[0]
+        ),
+        pltpu.make_async_copy(
+            send_hbm.at[pl.ds(far, 1)], picks.at[pl.ds(GROUPS, 1)], pick_sem.at[1]
+        ),
+        pltpu.make_async_copy(frac_hbm, frac_ref, pick_sem.at[2]),
+    ]
+    for copy in loads + others:
+        copy.start()
+
     barrier = pltpu.get_barrier_semaphore()
     for g in range(GROUPS):
         for jp in range(n_span):
@@ -57,15 +80,6 @@
                 pl.semaphore_signal(barrier, inc=1, device_id=(first + g, jp), device_id_type=MESH)
     pl.semaphore_signal(barrier, inc=1, device_id=(far, j), device_id_type=MESH)
 
-    near_picks = pltpu.make_async_copy(
-        send_hbm.at[pl.ds(first, GROUPS)], picks.at[pl.ds(0, GROUPS)], pick_sem.at[0]
-    )
-    far_picks = pltpu.make_async_copy(
-        send_hbm.at[pl.ds(far, 1)], picks.at[pl.ds(GROUPS, 1)], pick_sem.at[1]
-    )
-    near_picks.start()
-    far_picks.start()
-
     def relayout(xb, carry):
         for dx in range(2):
             for tile in range(CY // 8):
@@ -75,12 +89,12 @@
                     packed_ref[pl.ds(base + VARS + c, 8, ROW), :] = prev_ref[c, 2 * xb + dx, tile * 8:tile * 8 + 8, :]
         return carry
 
-    lax.fori_loop(0, BX, relayout, 0)
-    near_picks.wait()
-    far_picks.wait()
-
-    rows_near = jnp.minimum(i + REACH, n_stream - 1) - jnp.maximum(i - REACH, 0) + 1
-    pl.semaphore_wait(barrier, rows_near * n_span)
+    for part in range(PARTS):
+        loads[2 * part].wait()
+        loads[2 * part + 1].wait()
+        lax.fori_loop(part * BX // PARTS, (part + 1) * BX // PARTS, relayout, 0)
+    for copy in others:
+        copy.wait()
 
     half = lanes((ROW, 128)) < 64
     pair = lanes((BRICK, 128)) // 2
@@ -119,26 +133,42 @@
             device_id=(first + p // n_span, p % n_span), device_id_type=MESH,
         )
 
-    pack(far_slot, GROUPS, j * SLOT)
-    far_copy().start()
+    def start_near(g, jp):
+        @pl.when(is_partner(g, jp))
+        def _():
+            near_copy(g * n_span + jp, g, jp).start()
+
+    rows_near = jnp.minimum(i + REACH, n_stream - 1) - jnp.maximum(i - REACH, 0) + 1
+
+    def column(n):
+        return lax.rem(j + jnp.where(n == 0, 2, jnp.where(n == 1, 1, jnp.where(n == 2, 3, 0))), n_span)
 
     def send(n, carry):
-        turn = n // 2
-        g = jnp.where(n == 2 * turn, turn, GROUPS - 1 - turn)
-        t = first + g
-
-        @pl.when((t >= i - REACH) & (t <= i + REACH))
-        def _():
-            for jp in range(n_span):
-                pack(g * n_span + jp, g, jp * SLOT)
-            for jp in range(n_span):
-                @pl.when((t != i) | (jp != j))
-                def _():
-                    near_copy(g * n_span + jp, g, jp).start()
-
-        return carry
-
-    lax.fori_loop(0, GROUPS, send, 0)
+        jp = column(n)
+        for g in range(GROUPS):
+            pack(g * n_span + jp, g, jp * SLOT)
+
+        @pl.when(n == 0)
+        def _():
+            pack(far_slot, GROUPS, j * SLOT)
+
+        @pl.when(n == EARLY - 1)
+        def _():
+            pl.semaphore_wait(barrier, rows_near * n_span)
+            for early in range(EARLY):
+                for g in (0, 4, 1, 3, 2):
+                    start_near(g, column(early))
+                if early == 0:
+                    far_copy().start()
+
+        @pl.when(n >= EARLY)
+        def _():
+            for g in (0, 4, 1, 3, 2):
+                start_near(g, jp)
+
+        return carry
+
+    lax.fori_loop(0, n_span, send, 0)
     own = (i - first) * n_span + j
     arrived[own] = sending[own]
 
@@ -486,20 +516,24 @@
             jax.ShapeDtypeStruct((ROWS, CZ), F32),
             jax.ShapeDtypeStruct((slots, BRICK, 128), F32),
         ),
-        in_specs=[anywhere, vmem, vmem, vmem],
+        in_specs=[anywhere] * 4,
         out_specs=(vmem, vmem),
         scratch_shapes=[
             pltpu.SMEM((GROUPS + 1, 1, width), jnp.int32),
+            pltpu.VMEM((3, n_stream, width), F32),
+            pltpu.VMEM(q_now.shape, F32),
+            pltpu.VMEM(q_now.shape, F32),
             pltpu.VMEM((slots, ROW, 128), F32),
             pltpu.VMEM((slots, ROW, 128), F32),
-            pltpu.SemaphoreType.DMA((2,)),
+            pltpu.SemaphoreType.DMA((3,)),
+            pltpu.SemaphoreType.DMA((2 * PARTS,)),
             pltpu.SemaphoreType.DMA((slots,)),
             pltpu.SemaphoreType.DMA((slots,)),
         ],
         compiler_params=pltpu.CompilerParams(
-            collective_id=0, has_side_effects=True, vmem_limit_bytes=limit
+            collective_id=0, has_side_effects=True, vmem_limit_bytes=48 * 1024 * 1024
         ),
-    )(sending, offsets, q_now, q_prev)
+    )(*(pltpu.with_memory_space_constraint(x, pltpu.HBM) for x in (sending, offsets, q_now, q_prev)))
     shape = jax.ShapeDtypeStruct(q_now.shape, F32)
     now, older = pl.pallas_call(
         functools.partial(place_kernel, n_stream, n_span),

time: 42.7 us -> 36.7 us (0.86)
  the two profiles are of different devices: /device:TPU:7 before, /device:TPU:96 now
where the time goes in v3:
time: 36.7 us; the launch traced here: 36.6 us
  Pallas kernels  35.4 us (96%)
  local copies, waits for them, and re-layouts  1.15 us (3%)
    pallas_call x1, Pallas kernels, per_device(): pl.pallas_call(functools.partial(advance_kernel, n_stream, n_span), name=...  17.7 us
    pallas_call x1, Pallas kernels, per_device(): pl.pallas_call(functools.partial(exchange_kernel, n_stream, n_span), name...  12.8 us
    pallas_call x1, Pallas kernels, per_device(): pl.pallas_call(functools.partial(place_kernel, n_stream, n_span), name='p...  4.85 us
    unnamed x6, local copies, waits for them, and re-layouts  1.07 us

profile of v3, /device:TPU:96, one launch (start us, length us, event | category | flops | bytes accessed | tf_op | source)
XLA Modules:
  0.0 36.6 jit_solution(15580823635527764820)
XLA Ops:
  0.0 0.0 copy-start
  0.0 12.8 %exchange.1 = (f32[5120,128]{1,0:T(8,128)S(1)}, f32[21,40,128]{2,1,0:T(8,128)S(1)}) custom-call(s32[32,1,128]{2,1,0:T(1,128)} %bitcast.5, f32[3,32,128]{2,1,0:T(8,128)} %bitcast.4, f32[5,16,32,128]{3,2,1,0:T(8,128)} %now_hbm.1, f32[5,16,32,128]{3,2,1,0:T(8,128)} %prev_hbm.1), custom_call_target="tpu_custom_call" | custom-call | tf_op jit(solution)/shard_map/exchange/pallas_call | solution.py:512
  12.8 0.0 copy-done
  12.8 0.0 copy-start.1
  12.9 4.8 %place.1 = (f32[5,16,32,128]{3,2,1,0:T(8,128)S(1)}, f32[5,16,32,128]{3,2,1,0:T(8,128)S(1)}) custom-call(s32[32,1,128]{2,1,0:T(1,128)S(1)} %bitcast.3, f32[5120,128]{1,0:T(8,128)S(1)} %get-tuple-element.9.packed_hbm, f32[21,40,128]{2,1,0:T(8,128)S(1)} %get-tuple-element.10.fresh_ref), custom_call_target="tpu_custom_call" | custom-call | tf_op jit(solution)/shard_map/place/pallas_call | solution.py:538
  17.7 0.0 copy-done.1
  17.7 0.1 reshape.12.jac
  17.8 17.7 %advance.1 = f32[5,16,32,128]{3,2,1,0:T(8,128)S(1)} custom-call(f32[75]{0:T(128)S(1)} %reshape.12.jac, f32[5,16,32,128]{3,2,1,0:T(8,128)S(1)} %get-tuple-element.11.q_hbm, f32[5,16,32,128]{3,2,1,0:T(8,128)S(1)} %get-tuple-element.12.old_ref), custom_call_target="tpu_custom_call" | custom-call | tf_op jit(solution)/shard_map/advance/pallas_call | solution.py:551
  35.5 1.1 %copy.10 = f32[5,16,32,128]{3,2,1,0:T(8,128)} copy(f32[5,16,32,128]{3,2,1,0:T(8,128)S(1)} %advance.1) | data formatting | bytes 2621440
  (1 shorter events, 0.0 us)
Async XLA Ops:
  0.0 12.8 %copy-start = (s32[1,4096]{1,0:T(1,128)S(1)}, s32[1,4096]{1,0:T(1,128)}, u32[]{:S(2)}) copy-start(s32[1,4096]{1,0:T(1,128)} %param.11) | copy-start | bytes 49156
  12.8 4.9 %copy-start.1 = (f32[3,5,5]{2,0,1:T(4,128)S(1)}, f32[3,5,5]{2,0,1:T(4,128)}, u32[]{:S(2)}) copy-start(f32[3,5,5]{2,0,1:T(4,128)} %param.8) | copy-start | bytes 904

commit v4 on v3

--- a/solution.py
+++ b/solution.py
@@ -15,6 +15,7 @@
 REACH = 2
 PARTS = 4
 EARLY = 2
+BATCH = 4
 GROUPS = 2 * REACH + 1
 CX, CY, CZ = 16, 32, 128
 BX, BY = CX // 2, CY // 2
@@ -322,117 +323,173 @@
 
     load.wait()
 
-    def column(ref, width, c, x, y):
+    def flat_rows(ref, width, c, x, y, count):
         planes = CX + 2 * width
         flat = ref.reshape(VARS * planes * WY, CZ)
-        return flat, pl.ds((c * planes + width + x) * WY + PAD + y, 8, WY)
-
-    def pack(ref, out, width, side):
+        return flat, pl.ds((c * planes + width + x) * WY + PAD + y, count, WY)
+
+    def pack_near(side):
         for c in range(VARS):
-            for m in range(width):
+            for m in range(NEAR):
                 for x in range(0, CX, 8):
-                    flat, rows = column(ref, width, c, x, m if side == 2 else CY - width + m)
-                    out[side - 2, c, m, x:x + 8, :] = flat[rows, :]
-
-    def unpack(ref, held, width, side):
+                    flat, rows = flat_rows(wide, NEAR, c, x, m if side == 2 else CY - NEAR + m, 8)
+                    y_near_out[side - 2, c, m, x:x + 8, :] = flat[rows, :]
+
+    def unpack_near(side):
         for c in range(VARS):
-            for m in range(width):
+            for m in range(NEAR):
                 for x in range(0, CX, 8):
-                    flat, rows = column(ref, width, c, x, m - width if side == 2 else CY + m)
-                    flat[rows, :] = held[side - 2, c, m, x:x + 8, :]
-
-    def copy(ref, out, held, width, side, send, recv):
+                    flat, rows = flat_rows(wide, NEAR, c, x, m - NEAR if side == 2 else CY + m, 8)
+                    flat[rows, :] = y_near_in[side - 2, c, m, x:x + 8, :]
+
+    pieces = (((4, 8, 0),), ((0, 4, 0), (12, 4, 4)))
+
+    def pack_far(side, part):
+        for c in range(VARS):
+            for m in range(FAR):
+                for x, count, at in pieces[part]:
+                    flat, rows = flat_rows(pre, FAR, c, x, m if side == 2 else CY - FAR + m, count)
+                    y_far_out[side - 2, part, c, m, at:at + count, :] = flat[rows, :]
+
+    def unpack_far(side, part):
+        for c in range(VARS):
+            for m in range(FAR):
+                for x, count, at in pieces[part]:
+                    flat, rows = flat_rows(pre, FAR, c, x, m - FAR if side == 2 else CY + m, count)
+                    flat[rows, :] = y_far_in[side - 2, part, c, m, at:at + count, :]
+
+    def near(side, part):
         if side == 0:
-            src = ref.at[:, width:2 * width, PAD:PAD + CY, :]
-            dst = ref.at[:, width + CX:2 * width + CX, PAD:PAD + CY, :]
+            src = wide.at[:, NEAR:2 * NEAR, PAD:PAD + CY, :]
+            dst = wide.at[:, NEAR + CX:2 * NEAR + CX, PAD:PAD + CY, :]
         elif side == 1:
-            src = ref.at[:, CX:width + CX, PAD:PAD + CY, :]
-            dst = ref.at[:, 0:width, PAD:PAD + CY, :]
+            src = wide.at[:, CX:NEAR + CX, PAD:PAD + CY, :]
+            dst = wide.at[:, 0:NEAR, PAD:PAD + CY, :]
         else:
-            src = out.at[side - 2]
-            dst = held.at[3 - side]
+            src = y_near_out.at[side - 2]
+            dst = y_near_in.at[3 - side]
         return pltpu.make_async_remote_copy(
-            src_ref=src, dst_ref=dst, send_sem=send.at[side], recv_sem=recv.at[side ^ 1],
+            src_ref=src, dst_ref=dst, send_sem=near_send.at[side], recv_sem=near_recv.at[side ^ 1],
             device_id=ids[side], device_id_type=MESH,
         )
 
-    def near(side):
-        return copy(wide, y_near_out, y_near_in, NEAR, side, near_send, near_recv)
-
-    def far(side):
-        return copy(pre, y_far_out, y_far_in, FAR, side, far_send, far_recv)
-
-    def start(make, side):
+    inner = (NEAR, FAR)
+    outer = (0, NEAR)
+    x_parts = ((inner, (8, 24)), (inner, (0, 8)), (inner, (24, CY)), (outer, (0, CY)))
+
+    def far(side, part):
+        if side < 2:
+            (low, high), (top, bottom) = x_parts[part]
+            if side == 1:
+                low, high = CX - high, CX - low
+            shift = CX if side == 0 else -CX
+            rows = slice(PAD + top, PAD + bottom)
+            src = pre.at[:, FAR + low:FAR + high, rows, :]
+            dst = pre.at[:, FAR + low + shift:FAR + high + shift, rows, :]
+        else:
+            src = y_far_out.at[side - 2, part]
+            dst = y_far_in.at[3 - side, part]
+        return pltpu.make_async_remote_copy(
+            src_ref=src, dst_ref=dst, send_sem=far_send.at[side, part], recv_sem=far_recv.at[side ^ 1, part],
+            device_id=ids[side], device_id_type=MESH,
+        )
+
+    def start(make, side, part=0):
         @pl.when(has[side])
         def _():
-            make(side).start()
-
-    def finish_recv(make, side):
+            make(side, part).start()
+
+    def finish_recv(make, side, part=0):
         @pl.when(has[side])
         def _():
-            make(side ^ 1).wait_recv()
-
-    def finish_send(make, side):
+            make(side ^ 1, part).wait_recv()
+
+    def finish_send(make, side, part=0):
         @pl.when(has[side])
         def _():
-            make(side).wait_send()
+            make(side, part).wait_send()
 
     expected = sum(jnp.where(flag, 1, 0) for flag in has)
+    for side in (2, 3):
+        pack_near(side)
     pl.semaphore_wait(barrier, expected)
-    start(near, 0)
-    start(near, 1)
-    for side in (2, 3):
-        pack(wide, y_near_out, NEAR, side)
+    for side in range(4):
         start(near, side)
 
     slope = band(((1, 8.0), (-1, -8.0), (2, -1.0), (-2, 1.0)))
 
-    def base_plane(x, carry):
-        q = wide[:, NEAR + x, PAD:PAD + CY, :]
-        dz = along_z(q.reshape(VARS * CY, CZ), slope).reshape(VARS, CY, CZ) * (-1.0 / 36.0)
+    def base_planes(n, carry):
+        x = n * BATCH
+        q = wide[:, pl.ds(NEAR + x, BATCH), PAD:PAD + CY, :]
+        dz = along_z(q.reshape(VARS * BATCH * CY, CZ), slope).reshape(VARS, BATCH, CY, CZ)
+        dz = dz * (-1.0 / 36.0)
         for v in range(VARS):
-            total = (4.0 * q[v] - old_ref[v, x]) * (1.0 / 3.0)
+            total = (4.0 * q[v] - old_ref[v, pl.ds(x, BATCH)]) * (1.0 / 3.0)
             for w in range(VARS):
                 total = total + jac[50 + 5 * v + w] * dz[w]
-            pre[v, FAR + x, PAD:PAD + CY, :] = total
-        return carry
-
-    lax.fori_loop(0, CX, base_plane, 0)
-
-    for side in range(4):
+            pre[v, pl.ds(FAR + x, BATCH), PAD:PAD + CY, :] = total
+        return carry
+
+    lax.fori_loop(0, CX // BATCH, base_planes, 0)
+
+    def rate_tile(x, tile):
+        y = PAD + 8 * tile
+        dx, dy = [], []
+        for w in range(VARS):
+            def at(sx, sy):
+                return wide[w, NEAR + x + sx, y + sy:y + sy + 8, :]
+
+            dx.append((at(1, 0) - at(-1, 0)) * (-8.0 / 36.0) + (at(2, 0) - at(-2, 0)) * (1.0 / 36.0))
+            dy.append((at(0, 1) - at(0, -1)) * (-8.0 / 36.0) + (at(0, 2) - at(0, -2)) * (1.0 / 36.0))
+        for v in range(VARS):
+            total = pre[v, FAR + x, y:y + 8, :]
+            for w in range(VARS):
+                total = total + jac[5 * v + w] * dx[w]
+                total = total + jac[25 + 5 * v + w] * dy[w]
+            pre[v, FAR + x, y:y + 8, :] = total
+
+    def middle_planes(tiles):
+        def step(n, carry):
+            for x in (NEAR + 2 * n, NEAR + 2 * n + 1):
+                for tile in tiles:
+                    rate_tile(x, tile)
+            return carry
+
+        return step
+
+    pairs = CX // 2 - NEAR
+    lax.fori_loop(0, pairs, middle_planes((1, 2)), 0)
+    start(far, 0, 0)
+    start(far, 1, 0)
+    for side in (2, 3):
         finish_recv(near, side)
 
+        @pl.when(has[side])
+        def _():
+            unpack_near(side)
+
+    lax.fori_loop(0, pairs, middle_planes((0, 3)), 0)
+    for part in (1, 2):
+        start(far, 0, part)
+        start(far, 1, part)
     for side in (2, 3):
-        @pl.when(has[side])
-        def _():
-            unpack(wide, y_near_in, NEAR, side)
-
-    def rate_plane(x, carry):
-        for tile in range(CY // 8):
-            y = PAD + 8 * tile
-            dx, dy = [], []
-            for w in range(VARS):
-                def at(sx, sy):
-                    return wide[w, NEAR + x + sx, y + sy:y + sy + 8, :]
-
-                dx.append((at(1, 0) - at(-1, 0)) * (-8.0 / 36.0) + (at(2, 0) - at(-2, 0)) * (1.0 / 36.0))
-                dy.append((at(0, 1) - at(0, -1)) * (-8.0 / 36.0) + (at(0, 2) - at(0, -2)) * (1.0 / 36.0))
-            for v in range(VARS):
-                total = pre[v, FAR + x, y:y + 8, :]
-                for w in range(VARS):
-                    total = total + jac[5 * v + w] * dx[w]
-                    total = total + jac[25 + 5 * v + w] * dy[w]
-                pre[v, FAR + x, y:y + 8, :] = total
-        return carry
-
-    lax.fori_loop(0, FAR, rate_plane, 0)
-    start(far, 0)
-    lax.fori_loop(CX - FAR, CX, rate_plane, 0)
-    start(far, 1)
-    lax.fori_loop(FAR, CX - FAR, rate_plane, 0)
+        pack_far(side, 0)
+        start(far, side, 0)
+    for side in (0, 1):
+        finish_recv(near, side)
+
+    def outer_plane(n, carry):
+        for x in (n, CX - NEAR + n):
+            for tile in range(CY // 8):
+                rate_tile(x, tile)
+        return carry
+
+    lax.fori_loop(0, NEAR, outer_plane, 0)
+    start(far, 0, 3)
+    start(far, 1, 3)
     for side in (2, 3):
-        pack(pre, y_far_out, FAR, side)
-        start(far, side)
+        pack_far(side, 1)
+        start(far, side, 1)
 
     tenth = band(tuple((o, TAPS[abs(o)]) for o in range(-5, 6)))
 
@@ -447,19 +504,21 @@
             total = total + (TAPS[m] * SCALE) * (at(m) + at(-m))
         return total
 
-    def first_plane(x, carry):
-        p = pre[:, FAR + x, PAD:PAD + CY, :]
-        fz = along_z(p.reshape(VARS * CY, CZ), tenth).reshape(VARS, CY, CZ)
+    def first_planes(n, carry):
+        x = n * BATCH
+        p = pre[:, pl.ds(FAR + x, BATCH), PAD:PAD + CY, :]
+        fz = along_z(p.reshape(VARS * BATCH * CY, CZ), tenth).reshape(VARS, BATCH, CY, CZ)
         total = p + SCALE * fz
         for c in range(VARS):
-            for tile in range(CY // 8):
-                part = total[c, 8 * tile:8 * tile + 8]
-                if tile in (1, 2):
-                    part = part + filter_y(x, c, tile)
-                out_ref[c, x, 8 * tile:8 * tile + 8, :] = part
-        return carry
-
-    lax.fori_loop(0, CX, first_plane, 0)
+            for b in range(BATCH):
+                for tile in range(CY // 8):
+                    part = total[c, b, 8 * tile:8 * tile + 8]
+                    if tile in (1, 2):
+                        part = part + filter_y(x + b, c, tile)
+                    out_ref[c, x + b, 8 * tile:8 * tile + 8, :] = part
+        return carry
+
+    lax.fori_loop(0, CX // BATCH, first_planes, 0)
 
     def filter_x(x, carry):
         for c in range(VARS):
@@ -477,15 +536,17 @@
 
     lax.fori_loop(FAR, CX - FAR, filter_x, 0)
     for side in (0, 1):
-        finish_recv(far, side)
+        for part in range(4):
+            finish_recv(far, side, part)
     lax.fori_loop(0, FAR, filter_x, 0)
     lax.fori_loop(CX - FAR, CX, filter_x, 0)
     for side in (2, 3):
-        finish_recv(far, side)
-
-        @pl.when(has[side])
-        def _():
-            unpack(pre, y_far_in, FAR, side)
+        for part in range(2):
+            finish_recv(far, side, part)
+
+            @pl.when(has[side])
+            def _():
+                unpack_far(side, part)
 
     def edge_plane(x, carry):
         for c in range(VARS):
@@ -497,7 +558,8 @@
     lax.fori_loop(0, CX, edge_plane, 0)
     for side in range(4):
         finish_send(near, side)
-        finish_send(far, side)
+        for part in range(4 if side < 2 else 2):
+            finish_send(far, side, part)
 
 
 def per_device(n_stream, n_span, q_now, q_prev, jacobians, fractions, send_blocks, recv_blocks):
@@ -559,13 +621,13 @@
             pltpu.VMEM((VARS, CX + 2 * FAR, WY, CZ), F32),
             pltpu.VMEM((2, VARS, NEAR, CX, CZ), F32),
             pltpu.VMEM((2, VARS, NEAR, CX, CZ), F32),
-            pltpu.VMEM((2, VARS, FAR, CX, CZ), F32),
-            pltpu.VMEM((2, VARS, FAR, CX, CZ), F32),
+            pltpu.VMEM((2, 2, VARS, FAR, CX // 2, CZ), F32),
+            pltpu.VMEM((2, 2, VARS, FAR, CX // 2, CZ), F32),
             pltpu.SemaphoreType.DMA,
             pltpu.SemaphoreType.DMA((4,)),
             pltpu.SemaphoreType.DMA((4,)),
-            pltpu.SemaphoreType.DMA((4,)),
-            pltpu.SemaphoreType.DMA((4,)),
+            pltpu.SemaphoreType.DMA((4, 4)),
+            pltpu.SemaphoreType.DMA((4, 4)),
         ],
         compiler_params=pltpu.CompilerParams(
             collective_id=1, has_side_effects=True, vmem_limit_bytes=limit

time: 36.7 us -> 33.9 us (0.924)
  the two profiles are of different devices: /device:TPU:96 before, /device:TPU:7 now
where the time goes in v4:
time: 33.9 us; the launch traced here: 33.6 us
  Pallas kernels  32.4 us (96%)
  local copies, waits for them, and re-layouts  1.15 us (3%)
    pallas_call x1, Pallas kernels, per_device(): pl.pallas_call(functools.partial(advance_kernel, n_stream, n_span), name=...  14.8 us
    pallas_call x1, Pallas kernels, per_device(): pl.pallas_call(functools.partial(exchange_kernel, n_stream, n_span), name...  12.7 us
    pallas_call x1, Pallas kernels, per_device(): pl.pallas_call(functools.partial(place_kernel, n_stream, n_span), name='p...  4.85 us
    unnamed x6, local copies, waits for them, and re-layouts  1.07 us

profile of v4, /device:TPU:7, one launch (start us, length us, event | category | flops | bytes accessed | tf_op | source)
XLA Modules:
  0.0 33.6 jit_solution(17362795523567490174)
XLA Ops:
  0.0 0.0 copy-start
  0.0 12.7 %exchange.1 = (f32[5120,128]{1,0:T(8,128)S(1)}, f32[21,40,128]{2,1,0:T(8,128)S(1)}) custom-call(s32[32,1,128]{2,1,0:T(1,128)} %bitcast.5, f32[3,32,128]{2,1,0:T(8,128)} %bitcast.4, f32[5,16,32,128]{3,2,1,0:T(8,128)} %now_hbm.1, f32[5,16,32,128]{3,2,1,0:T(8,128)} %prev_hbm.1), custom_call_target="tpu_custom_call" | custom-call | tf_op jit(solution)/shard_map/exchange/pallas_call | solution.py:574
  12.7 0.0 copy-done
  12.7 0.0 copy-start.1
  12.7 4.8 %place.1 = (f32[5,16,32,128]{3,2,1,0:T(8,128)S(1)}, f32[5,16,32,128]{3,2,1,0:T(8,128)S(1)}) custom-call(s32[32,1,128]{2,1,0:T(1,128)S(1)} %bitcast.3, f32[5120,128]{1,0:T(8,128)S(1)} %get-tuple-element.9.packed_hbm, f32[21,40,128]{2,1,0:T(8,128)S(1)} %get-tuple-element.10.fresh_ref), custom_call_target="tpu_custom_call" | custom-call | tf_op jit(solution)/shard_map/place/pallas_call | solution.py:600
  17.6 0.0 copy-done.1
  17.6 0.1 reshape.12.jac
  17.7 14.8 %advance.1 = f32[5,16,32,128]{3,2,1,0:T(8,128)S(1)} custom-call(f32[75]{0:T(128)S(1)} %reshape.12.jac, f32[5,16,32,128]{3,2,1,0:T(8,128)S(1)} %get-tuple-element.11.q_hbm, f32[5,16,32,128]{3,2,1,0:T(8,128)S(1)} %get-tuple-element.12.old_ref), custom_call_target="tpu_custom_call" | custom-call | tf_op jit(solution)/shard_map/advance/pallas_call | solution.py:613
  32.5 1.1 %copy.10 = f32[5,16,32,128]{3,2,1,0:T(8,128)} copy(f32[5,16,32,128]{3,2,1,0:T(8,128)S(1)} %advance.1) | data formatting | bytes 2621440
  (1 shorter events, 0.0 us)
Async XLA Ops:
  0.0 12.7 %copy-start = (s32[1,4096]{1,0:T(1,128)S(1)}, s32[1,4096]{1,0:T(1,128)}, u32[]{:S(2)}) copy-start(s32[1,4096]{1,0:T(1,128)} %param.11) | copy-start | bytes 49156
  12.7 4.9 %copy-start.1 = (f32[3,5,5]{2,0,1:T(4,128)S(1)}, f32[3,5,5]{2,0,1:T(4,128)}, u32[]{:S(2)}) copy-start(f32[3,5,5]{2,0,1:T(4,128)} %param.8) | copy-start | bytes 904

commit v5 on v4

--- a/solution.py
+++ b/solution.py
@@ -131,7 +131,7 @@
         return pltpu.make_async_remote_copy(
             src_ref=sending.at[p], dst_ref=arrived.at[p],
             send_sem=send_sem.at[p], recv_sem=recv_sem.at[p],
-            device_id=(first + p // n_span, p % n_span), device_id_type=MESH,
+            device_id=(first + p // n_span, lax.rem(p, n_span)), device_id_type=MESH,
         )
 
     def start_near(g, jp):
@@ -183,8 +183,6 @@
         chosen = jnp.where(source == wanted, 1.0, 0.0).astype(F32)
         return jnp.dot(table, chosen, precision=lax.Precision.HIGHEST, preferred_element_type=F32)
 
-    spreads = [spread(jp) for jp in range(n_span)]
-    far_spread = spread(j)
     even = lanes((CHANS, 128)) % 2 == 0
     low_half = lanes((CHANS, 128)) < 64
 
@@ -201,16 +199,19 @@
         fresh_ref[p, 0:ROW, :] = both
         fresh_ref[p, ROW:BRICK, :] = pltpu.roll(both, 64, 1)
 
-    for p in range(near_count):
-        @pl.when(is_partner(p // n_span, p % n_span))
-        def _():
-            arrival(p).wait_recv()
-
-    far_copy().wait_recv()
-    for p in range(near_count):
-        g, jp = p // n_span, p % n_span
-        finish(p, *(spreads[jp][6 * d + g:6 * d + g + 1] for d in range(3)))
-    finish(far_slot, *(far_spread[6 * d + GROUPS:6 * d + GROUPS + 1] for d in range(3)))
+    for n in range(n_span):
+        jp = column(n)
+        shares = spread(jp)
+        if n == 1:
+            far_shares = spread(j)
+            far_copy().wait_recv()
+            finish(far_slot, *(far_shares[6 * d + GROUPS:6 * d + GROUPS + 1] for d in range(3)))
+        for g in range(GROUPS):
+            @pl.when(is_partner(g, jp))
+            def _():
+                arrival(g * n_span + jp).wait_recv()
+        for g in range(GROUPS):
+            finish(g * n_span + jp, *(shares[6 * d + g:6 * d + g + 1] for d in range(3)))
     for p in range(near_count):
         @pl.when(is_partner(p // n_span, p % n_span))
         def _():
@@ -313,13 +314,16 @@
         def _():
             ref[:, width + CX:planes, :, :] = jnp.zeros((VARS, width, WY, CZ), F32)
 
-        @pl.when(~has[2])
-        def _():
-            ref[:, width:width + CX, 0:PAD, :] = jnp.zeros((VARS, CX, PAD, CZ), F32)
-
-        @pl.when(~has[3])
-        def _():
-            ref[:, width:width + CX, PAD + CY:WY, :] = jnp.zeros((VARS, CX, PAD, CZ), F32)
+    @pl.when(~has[2])
+    def _():
+        wide[:, NEAR:NEAR + CX, 0:PAD, :] = jnp.zeros((VARS, CX, PAD, CZ), F32)
+
+    @pl.when(~has[3])
+    def _():
+        wide[:, NEAR:NEAR + CX, PAD + CY:WY, :] = jnp.zeros((VARS, CX, PAD, CZ), F32)
+
+    for edge in (0, PAD + CY):
+        pre[:, FAR:FAR + CX, edge:edge + PAD, :] = jnp.zeros((VARS, CX, PAD, CZ), F32)
 
     load.wait()
 
@@ -351,12 +355,39 @@
                     flat, rows = flat_rows(pre, FAR, c, x, m if side == 2 else CY - FAR + m, count)
                     y_far_out[side - 2, part, c, m, at:at + count, :] = flat[rows, :]
 
-    def unpack_far(side, part):
+    out_rows = out_ref.reshape(VARS * CX * CY, CZ)
+
+    def add_far_y(side, part):
         for c in range(VARS):
-            for m in range(FAR):
+            held = [y_far_in[side - 2, part, c, m] for m in range(FAR)]
+            for r in range(FAR):
+                total = None
+                for m in range(r, FAR) if side == 2 else range(r + 1):
+                    away = r + FAR - m if side == 2 else FAR + m - r
+                    term = (TAPS[away] * SCALE) * held[m]
+                    total = term if total is None else total + term
+                row = r if side == 2 else CY - FAR + r
                 for x, count, at in pieces[part]:
-                    flat, rows = flat_rows(pre, FAR, c, x, m - FAR if side == 2 else CY + m, count)
-                    flat[rows, :] = y_far_in[side - 2, part, c, m, at:at + count, :]
+                    rows = pl.ds((c * CX + x) * CY + row, count, CY)
+                    out_rows[rows, :] = out_rows[rows, :] + total[at:at + count]
+
+    def add_far_x(side):
+        def step(c, carry):
+            for tile in range(CY // 8):
+                y = PAD + 8 * tile
+                first_plane = 0 if side == 0 else FAR + CX
+                held = [pre[c, first_plane + m, y:y + 8, :] for m in range(FAR)]
+                for r in range(FAR):
+                    total = None
+                    for m in range(r, FAR) if side == 0 else range(r + 1):
+                        away = r + FAR - m if side == 0 else FAR + m - r
+                        term = (TAPS[away] * SCALE) * held[m]
+                        total = term if total is None else total + term
+                    x = r if side == 0 else CX - FAR + r
+                    out_ref[c, x, 8 * tile:8 * tile + 8, :] = out_ref[c, x, 8 * tile:8 * tile + 8, :] + total
+            return carry
+
+        return step
 
     def near(side, part):
         if side == 0:
@@ -512,50 +543,40 @@
         for c in range(VARS):
             for b in range(BATCH):
                 for tile in range(CY // 8):
-                    part = total[c, b, 8 * tile:8 * tile + 8]
-                    if tile in (1, 2):
-                        part = part + filter_y(x + b, c, tile)
+                    part = total[c, b, 8 * tile:8 * tile + 8] + filter_y(x + b, c, tile)
                     out_ref[c, x + b, 8 * tile:8 * tile + 8, :] = part
         return carry
 
     lax.fori_loop(0, CX // BATCH, first_planes, 0)
 
-    def filter_x(x, carry):
-        for c in range(VARS):
-            for tile in range(CY // 8):
-                y = PAD + 8 * tile
-
-                def at(sx):
-                    return pre[c, FAR + x + sx, y:y + 8, :]
-
-                total = out_ref[c, x, 8 * tile:8 * tile + 8, :] + (TAPS[0] * SCALE) * at(0)
+    def filter_x(c, carry):
+        for tile in range(CY // 8):
+            y = PAD + 8 * tile
+            line = [pre[c, FAR + x, y:y + 8, :] for x in range(CX)]
+            for x in range(CX):
+                total = out_ref[c, x, 8 * tile:8 * tile + 8, :] + (TAPS[0] * SCALE) * line[x]
                 for m in range(1, 6):
-                    total = total + (TAPS[m] * SCALE) * (at(m) + at(-m))
+                    near_by = [line[x + o] for o in (m, -m) if 0 <= x + o < CX]
+                    total = total + (TAPS[m] * SCALE) * sum(near_by[1:], near_by[0])
                 out_ref[c, x, 8 * tile:8 * tile + 8, :] = total
         return carry
 
-    lax.fori_loop(FAR, CX - FAR, filter_x, 0)
+    lax.fori_loop(0, VARS, filter_x, 0)
+
+    def receive_far_y(part):
+        for side in (2, 3):
+            finish_recv(far, side, part)
+
+            @pl.when(has[side])
+            def _():
+                add_far_y(side, part)
+
+    receive_far_y(0)
     for side in (0, 1):
         for part in range(4):
             finish_recv(far, side, part)
-    lax.fori_loop(0, FAR, filter_x, 0)
-    lax.fori_loop(CX - FAR, CX, filter_x, 0)
-    for side in (2, 3):
-        for part in range(2):
-            finish_recv(far, side, part)
-
-            @pl.when(has[side])
-            def _():
-                unpack_far(side, part)
-
-    def edge_plane(x, carry):
-        for c in range(VARS):
-            for tile in (0, CY // 8 - 1):
-                rows = pl.ds(8 * tile, 8)
-                out_ref[c, x, rows, :] = out_ref[c, x, rows, :] + filter_y(x, c, tile)
-        return carry
-
-    lax.fori_loop(0, CX, edge_plane, 0)
+        lax.fori_loop(0, VARS, add_far_x(side), 0)
+    receive_far_y(1)
     for side in range(4):
         finish_send(near, side)
         for part in range(4 if side < 2 else 2):

time: 33.9 us -> 32.9 us (0.971)
  Pallas kernels: 32.4 us -> 31.6 us
    pallas_call x1, Pallas kernels: 14.8 us -> 14 us  [per_device(): pl.pallas_call(functools.partial(advance_kernel, n_stream, n_span), name=...]
where the time goes in v5:
time: 32.9 us; the launch traced here: 32.8 us
  Pallas kernels  31.6 us (96%)
  local copies, waits for them, and re-layouts  1.15 us (3%)
    pallas_call x1, Pallas kernels, per_device(): pl.pallas_call(functools.partial(advance_kernel, n_stream, n_span), name=...  14 us
    pallas_call x1, Pallas kernels, per_device(): pl.pallas_call(functools.partial(exchange_kernel, n_stream, n_span), name...  12.8 us
    pallas_call x1, Pallas kernels, per_device(): pl.pallas_call(functools.partial(place_kernel, n_stream, n_span), name='p...  4.85 us
    unnamed x6, local copies, waits for them, and re-layouts  1.07 us

profile of v5, /device:TPU:7, one launch (start us, length us, event | category | flops | bytes accessed | tf_op | source)
XLA Modules:
  0.0 32.8 jit_solution(18198835531427804525)
XLA Ops:
  0.0 0.0 copy-start
  0.0 12.8 %exchange.1 = (f32[5120,128]{1,0:T(8,128)S(1)}, f32[21,40,128]{2,1,0:T(8,128)S(1)}) custom-call(s32[32,1,128]{2,1,0:T(1,128)} %bitcast.5, f32[3,32,128]{2,1,0:T(8,128)} %bitcast.4, f32[5,16,32,128]{3,2,1,0:T(8,128)} %now_hbm.1, f32[5,16,32,128]{3,2,1,0:T(8,128)} %prev_hbm.1), custom_call_target="tpu_custom_call" | custom-call | tf_op jit(solution)/shard_map/exchange/pallas_call | solution.py:595
  12.8 0.0 copy-done
  12.8 0.0 copy-start.1
  12.8 4.8 %place.1 = (f32[5,16,32,128]{3,2,1,0:T(8,128)S(1)}, f32[5,16,32,128]{3,2,1,0:T(8,128)S(1)}) custom-call(s32[32,1,128]{2,1,0:T(1,128)S(1)} %bitcast.3, f32[5120,128]{1,0:T(8,128)S(1)} %get-tuple-element.9.packed_hbm, f32[21,40,128]{2,1,0:T(8,128)S(1)} %get-tuple-element.10.fresh_ref), custom_call_target="tpu_custom_call" | custom-call | tf_op jit(solution)/shard_map/place/pallas_call | solution.py:621
  17.6 0.0 copy-done.1
  17.7 0.1 reshape.12.jac
  17.8 14.0 %advance.1 = f32[5,16,32,128]{3,2,1,0:T(8,128)S(1)} custom-call(f32[75]{0:T(128)S(1)} %reshape.12.jac, f32[5,16,32,128]{3,2,1,0:T(8,128)S(1)} %get-tuple-element.11.q_hbm, f32[5,16,32,128]{3,2,1,0:T(8,128)S(1)} %get-tuple-element.12.old_ref), custom_call_target="tpu_custom_call" | custom-call | tf_op jit(solution)/shard_map/advance/pallas_call | solution.py:634
  31.7 1.1 %copy.10 = f32[5,16,32,128]{3,2,1,0:T(8,128)} copy(f32[5,16,32,128]{3,2,1,0:T(8,128)S(1)} %advance.1) | data formatting | bytes 2621440
  (1 shorter events, 0.0 us)
Async XLA Ops:
  0.0 12.8 %copy-start = (s32[1,4096]{1,0:T(1,128)S(1)}, s32[1,4096]{1,0:T(1,128)}, u32[]{:S(2)}) copy-start(s32[1,4096]{1,0:T(1,128)} %param.11) | copy-start | bytes 49156
  12.8 4.9 %copy-start.1 = (f32[3,5,5]{2,0,1:T(4,128)S(1)}, f32[3,5,5]{2,0,1:T(4,128)}, u32[]{:S(2)}) copy-start(f32[3,5,5]{2,0,1:T(4,128)} %param.8) | copy-start | bytes 904

commit v6 on v5

--- a/solution.py
+++ b/solution.py
@@ -314,15 +314,8 @@
         def _():
             ref[:, width + CX:planes, :, :] = jnp.zeros((VARS, width, WY, CZ), F32)
 
-    @pl.when(~has[2])
-    def _():
-        wide[:, NEAR:NEAR + CX, 0:PAD, :] = jnp.zeros((VARS, CX, PAD, CZ), F32)
-
-    @pl.when(~has[3])
-    def _():
-        wide[:, NEAR:NEAR + CX, PAD + CY:WY, :] = jnp.zeros((VARS, CX, PAD, CZ), F32)
-
     for edge in (0, PAD + CY):
+        wide[:, NEAR:NEAR + CX, edge:edge + PAD, :] = jnp.zeros((VARS, CX, PAD, CZ), F32)
         pre[:, FAR:FAR + CX, edge:edge + PAD, :] = jnp.zeros((VARS, CX, PAD, CZ), F32)
 
     load.wait()
@@ -339,27 +332,61 @@
                     flat, rows = flat_rows(wide, NEAR, c, x, m if side == 2 else CY - NEAR + m, 8)
                     y_near_out[side - 2, c, m, x:x + 8, :] = flat[rows, :]
 
-    def unpack_near(side):
+    def near_terms(low, inner, outer):
+        edge = inner * (8.0 / 36.0) - outer * (1.0 / 36.0)
+        second = inner * (-1.0 / 36.0)
+        return (edge, second) if low else (-edge, -second)
+
+    def add_near_y(side):
+        for x in range(0, CX, 8):
+            terms = []
+            for w in range(VARS):
+                held = [y_near_in[side - 2, w, m, x:x + 8, :] for m in range(NEAR)]
+                terms.append(near_terms(side == 2, *(reversed(held) if side == 2 else held)))
+            for k in range(NEAR):
+                for v in range(VARS):
+                    flat, rows = flat_rows(pre, FAR, v, x, k if side == 2 else CY - 1 - k, 8)
+                    total = flat[rows, :]
+                    for w in range(VARS):
+                        total = total + jac[25 + 5 * v + w] * terms[w][k]
+                    flat[rows, :] = total
+
+    def add_near_x(side):
+        def step(tile, carry):
+            rows = pl.ds(PAD + 8 * tile, 8)
+            terms = []
+            for w in range(VARS):
+                held = [wide[w, m if side == 0 else NEAR + CX + m, rows, :] for m in range(NEAR)]
+                terms.append(near_terms(side == 0, *(reversed(held) if side == 0 else held)))
+            for k in range(NEAR):
+                x = k if side == 0 else CX - 1 - k
+                for v in range(VARS):
+                    total = pre[v, FAR + x, rows, :]
+                    for w in range(VARS):
+                        total = total + jac[5 * v + w] * terms[w][k]
+                    pre[v, FAR + x, rows, :] = total
+            return carry
+
+        return step
+
+    inner_x, outer_x = ((4, 8, 0),), ((0, 4, 0), (12, 4, 4))
+    y_order = {2: (2, 3, 4, 0, 1), 3: (0, 1, 2, 3, 4)}
+    y_parts = ((0, 3), (3, 5), (5, 10))
+
+    def pack_far(side, part):
+        for at_plane in range(*y_parts[part]):
+            m = y_order[side][at_plane] if part < 2 else at_plane - FAR
+            for c in range(VARS):
+                for x, count, at in inner_x if part < 2 else outer_x:
+                    flat, rows = flat_rows(pre, FAR, c, x, m if side == 2 else CY - FAR + m, count)
+                    y_far_out[side - 2, at_plane, c, at:at + count, :] = flat[rows, :]
+
+    out_rows = out_ref.reshape(VARS * CX * CY, CZ)
+
+    def add_far_y(side, outer):
         for c in range(VARS):
-            for m in range(NEAR):
-                for x in range(0, CX, 8):
-                    flat, rows = flat_rows(wide, NEAR, c, x, m - NEAR if side == 2 else CY + m, 8)
-                    flat[rows, :] = y_near_in[side - 2, c, m, x:x + 8, :]
-
-    pieces = (((4, 8, 0),), ((0, 4, 0), (12, 4, 4)))
-
-    def pack_far(side, part):
-        for c in range(VARS):
-            for m in range(FAR):
-                for x, count, at in pieces[part]:
-                    flat, rows = flat_rows(pre, FAR, c, x, m if side == 2 else CY - FAR + m, count)
-                    y_far_out[side - 2, part, c, m, at:at + count, :] = flat[rows, :]
-
-    out_rows = out_ref.reshape(VARS * CX * CY, CZ)
-
-    def add_far_y(side, part):
-        for c in range(VARS):
-            held = [y_far_in[side - 2, part, c, m] for m in range(FAR)]
+            order = y_order[side ^ 1]
+            held = [y_far_in[side - 2, FAR + m if outer else order.index(m), c] for m in range(FAR)]
             for r in range(FAR):
                 total = None
                 for m in range(r, FAR) if side == 2 else range(r + 1):
@@ -367,7 +394,7 @@
                     term = (TAPS[away] * SCALE) * held[m]
                     total = term if total is None else total + term
                 row = r if side == 2 else CY - FAR + r
-                for x, count, at in pieces[part]:
+                for x, count, at in outer_x if outer else inner_x:
                     rows = pl.ds((c * CX + x) * CY + row, count, CY)
                     out_rows[rows, :] = out_rows[rows, :] + total[at:at + count]
 
@@ -418,8 +445,9 @@
             src = pre.at[:, FAR + low:FAR + high, rows, :]
             dst = pre.at[:, FAR + low + shift:FAR + high + shift, rows, :]
         else:
-            src = y_far_out.at[side - 2, part]
-            dst = y_far_in.at[3 - side, part]
+            low, high = y_parts[part]
+            src = y_far_out.at[side - 2, low:high]
+            dst = y_far_in.at[3 - side, low:high]
         return pltpu.make_async_remote_copy(
             src_ref=src, dst_ref=dst, send_sem=far_send.at[side, part], recv_sem=far_recv.at[side ^ 1, part],
             device_id=ids[side], device_id_type=MESH,
@@ -463,64 +491,67 @@
 
     lax.fori_loop(0, CX // BATCH, base_planes, 0)
 
-    def rate_tile(x, tile):
-        y = PAD + 8 * tile
+    def rate_tile(x, y, offsets):
         dx, dy = [], []
         for w in range(VARS):
             def at(sx, sy):
-                return wide[w, NEAR + x + sx, y + sy:y + sy + 8, :]
-
-            dx.append((at(1, 0) - at(-1, 0)) * (-8.0 / 36.0) + (at(2, 0) - at(-2, 0)) * (1.0 / 36.0))
+                return wide[w, NEAR + x + sx, pl.ds(y + sy, 8), :]
+
+            parts = [
+                at(o, 0) * ((-8.0 if abs(o) == 1 else 1.0) * (1.0 if o > 0 else -1.0) / 36.0) for o in offsets
+            ]
+            dx.append(sum(parts[1:], parts[0]))
             dy.append((at(0, 1) - at(0, -1)) * (-8.0 / 36.0) + (at(0, 2) - at(0, -2)) * (1.0 / 36.0))
         for v in range(VARS):
-            total = pre[v, FAR + x, y:y + 8, :]
+            total = pre[v, FAR + x, pl.ds(y, 8), :]
             for w in range(VARS):
                 total = total + jac[5 * v + w] * dx[w]
                 total = total + jac[25 + 5 * v + w] * dy[w]
-            pre[v, FAR + x, y:y + 8, :] = total
+            pre[v, FAR + x, pl.ds(y, 8), :] = total
 
     def middle_planes(tiles):
         def step(n, carry):
             for x in (NEAR + 2 * n, NEAR + 2 * n + 1):
                 for tile in tiles:
-                    rate_tile(x, tile)
+                    rate_tile(x, PAD + 8 * tile, (-2, -1, 1, 2))
             return carry
 
         return step
+
+    def outer_planes(tile, carry):
+        y = pl.multiple_of(PAD + 8 * tile, 8)
+        for x in (0, 1, CX - 2, CX - 1):
+            rate_tile(x, y, [o for o in (-2, -1, 1, 2) if 0 <= x + o < CX])
+        return carry
 
     pairs = CX // 2 - NEAR
     lax.fori_loop(0, pairs, middle_planes((1, 2)), 0)
     start(far, 0, 0)
     start(far, 1, 0)
+    lax.fori_loop(0, pairs, middle_planes((0, 3)), 0)
+    for side in (2, 3):
+        pack_far(side, 0)
+        start(far, side, 0)
+    lax.fori_loop(0, CY // 8, outer_planes, 0)
     for side in (2, 3):
         finish_recv(near, side)
 
         @pl.when(has[side])
         def _():
-            unpack_near(side)
-
-    lax.fori_loop(0, pairs, middle_planes((0, 3)), 0)
+            add_near_y(side)
+
+        pack_far(side, 1)
+        start(far, side, 1)
     for part in (1, 2):
         start(far, 0, part)
         start(far, 1, part)
-    for side in (2, 3):
-        pack_far(side, 0)
-        start(far, side, 0)
     for side in (0, 1):
         finish_recv(near, side)
-
-    def outer_plane(n, carry):
-        for x in (n, CX - NEAR + n):
-            for tile in range(CY // 8):
-                rate_tile(x, tile)
-        return carry
-
-    lax.fori_loop(0, NEAR, outer_plane, 0)
-    start(far, 0, 3)
-    start(far, 1, 3)
+        lax.fori_loop(0, CY // 8, add_near_x(side), 0)
+        start(far, side, 3)
     for side in (2, 3):
-        pack_far(side, 1)
-        start(far, side, 1)
+        pack_far(side, 2)
+        start(far, side, 2)
 
     tenth = band(tuple((o, TAPS[abs(o)]) for o in range(-5, 6)))
 
@@ -563,23 +594,24 @@
 
     lax.fori_loop(0, VARS, filter_x, 0)
 
-    def receive_far_y(part):
+    def receive_far_y(parts, outer):
         for side in (2, 3):
-            finish_recv(far, side, part)
+            for part in parts:
+                finish_recv(far, side, part)
 
             @pl.when(has[side])
             def _():
-                add_far_y(side, part)
-
-    receive_far_y(0)
+                add_far_y(side, outer)
+
+    receive_far_y((0, 1), False)
     for side in (0, 1):
         for part in range(4):
             finish_recv(far, side, part)
         lax.fori_loop(0, VARS, add_far_x(side), 0)
-    receive_far_y(1)
+    receive_far_y((2,), True)
     for side in range(4):
         finish_send(near, side)
-        for part in range(4 if side < 2 else 2):
+        for part in range(4 if side < 2 else 3):
             finish_send(far, side, part)
 
 
@@ -642,8 +674,8 @@
             pltpu.VMEM((VARS, CX + 2 * FAR, WY, CZ), F32),
             pltpu.VMEM((2, VARS, NEAR, CX, CZ), F32),
             pltpu.VMEM((2, VARS, NEAR, CX, CZ), F32),
-            pltpu.VMEM((2, 2, VARS, FAR, CX // 2, CZ), F32),
-            pltpu.VMEM((2, 2, VARS, FAR, CX // 2, CZ), F32),
+            pltpu.VMEM((2, 2 * FAR, VARS, CX // 2, CZ), F32),
+            pltpu.VMEM((2, 2 * FAR, VARS, CX // 2, CZ), F32),
             pltpu.SemaphoreType.DMA,
             pltpu.SemaphoreType.DMA((4,)),
             pltpu.SemaphoreType.DMA((4,)),

time: 32.9 us -> 32.6 us (level)
  no operation moved by 1% of the time
where the time goes in v6:
time: 32.6 us; the launch traced here: 32.5 us
  Pallas kernels  31.3 us (96%)
  local copies, waits for them, and re-layouts  1.15 us (4%)
    pallas_call x1, Pallas kernels, per_device(): pl.pallas_call(functools.partial(advance_kernel, n_stream, n_span), name=...  13.7 us
    pallas_call x1, Pallas kernels, per_device(): pl.pallas_call(functools.partial(exchange_kernel, n_stream, n_span), name...  12.8 us
    pallas_call x1, Pallas kernels, per_device(): pl.pallas_call(functools.partial(place_kernel, n_stream, n_span), name='p...  4.85 us
    unnamed x6, local copies, waits for them, and re-layouts  1.07 us

profile of v6, /device:TPU:7, one launch (start us, length us, event | category | flops | bytes accessed | tf_op | source)
XLA Modules:
  0.0 32.5 jit_solution(16280220187527680346)
XLA Ops:
  0.0 0.0 copy-start
  0.0 12.8 %exchange.1 = (f32[5120,128]{1,0:T(8,128)S(1)}, f32[21,40,128]{2,1,0:T(8,128)S(1)}) custom-call(s32[32,1,128]{2,1,0:T(1,128)} %bitcast.5, f32[3,32,128]{2,1,0:T(8,128)} %bitcast.4, f32[5,16,32,128]{3,2,1,0:T(8,128)} %now_hbm.1, f32[5,16,32,128]{3,2,1,0:T(8,128)} %prev_hbm.1), custom_call_target="tpu_custom_call" | custom-call | tf_op jit(solution)/shard_map/exchange/pallas_call | solution.py:627
  12.8 0.0 copy-done
  12.8 0.0 copy-start.1
  12.8 4.8 %place.1 = (f32[5,16,32,128]{3,2,1,0:T(8,128)S(1)}, f32[5,16,32,128]{3,2,1,0:T(8,128)S(1)}) custom-call(s32[32,1,128]{2,1,0:T(1,128)S(1)} %bitcast.3, f32[5120,128]{1,0:T(8,128)S(1)} %get-tuple-element.9.packed_hbm, f32[21,40,128]{2,1,0:T(8,128)S(1)} %get-tuple-element.10.fresh_ref), custom_call_target="tpu_custom_call" | custom-call | tf_op jit(solution)/shard_map/place/pallas_call | solution.py:653
  17.7 0.0 copy-done.1
  17.7 0.1 reshape.12.jac
  17.8 13.7 %advance.1 = f32[5,16,32,128]{3,2,1,0:T(8,128)S(1)} custom-call(f32[75]{0:T(128)S(1)} %reshape.12.jac, f32[5,16,32,128]{3,2,1,0:T(8,128)S(1)} %get-tuple-element.11.q_hbm, f32[5,16,32,128]{3,2,1,0:T(8,128)S(1)} %get-tuple-element.12.old_ref), custom_call_target="tpu_custom_call" | custom-call | tf_op jit(solution)/shard_map/advance/pallas_call | solution.py:666
  31.4 1.1 %copy.10 = f32[5,16,32,128]{3,2,1,0:T(8,128)} copy(f32[5,16,32,128]{3,2,1,0:T(8,128)S(1)} %advance.1) | data formatting | bytes 2621440
  (1 shorter events, 0.0 us)
Async XLA Ops:
  0.0 12.8 %copy-start = (s32[1,4096]{1,0:T(1,128)S(1)}, s32[1,4096]{1,0:T(1,128)}, u32[]{:S(2)}) copy-start(s32[1,4096]{1,0:T(1,128)} %param.11) | copy-start | bytes 49156
  12.8 4.9 %copy-start.1 = (f32[3,5,5]{2,0,1:T(4,128)S(1)}, f32[3,5,5]{2,0,1:T(4,128)}, u32[]{:S(2)}) copy-start(f32[3,5,5]{2,0,1:T(4,128)} %param.8) | copy-start | bytes 904

commit v7 on v6

--- a/solution.py
+++ b/solution.py
@@ -199,11 +199,12 @@
         fresh_ref[p, 0:ROW, :] = both
         fresh_ref[p, ROW:BRICK, :] = pltpu.roll(both, 64, 1)
 
+    all_shares = [spread(column(n)) for n in range(n_span)]
+    far_shares = all_shares[n_span - 1]
     for n in range(n_span):
         jp = column(n)
-        shares = spread(jp)
+        shares = all_shares[n]
         if n == 1:
-            far_shares = spread(j)
             far_copy().wait_recv()
             finish(far_slot, *(far_shares[6 * d + GROUPS:6 * d + GROUPS + 1] for d in range(3)))
         for g in range(GROUPS):
@@ -248,12 +249,9 @@
             base = pl.multiple_of((brick >> 6) * BRICK, 8)
             pltpu.store(work.at[pl.ds(base, BRICK), :], moved, mask=pair == mark)
 
-    def put_group(g, carry):
+    for g in range(GROUPS):
         for jp in range(n_span):
             put(g * n_span + jp, g, jp * SLOT)
-        return carry
-
-    lax.fori_loop(0, GROUPS, put_group, 0)
     put(near_count, GROUPS, j * SLOT)
 
     def relayout(xb, carry):

time: 32.6 us -> 32.3 us (level)
  Pallas kernels: 31.3 us -> 30.9 us
where the time goes in v7:
time: 32.3 us; the launch traced here: 32.1 us
  Pallas kernels  30.9 us (96%)
  local copies, waits for them, and re-layouts  1.15 us (4%)
    pallas_call x1, Pallas kernels, per_device(): pl.pallas_call(functools.partial(advance_kernel, n_stream, n_span), name=...  13.6 us
    pallas_call x1, Pallas kernels, per_device(): pl.pallas_call(functools.partial(exchange_kernel, n_stream, n_span), name...  12.7 us
    pallas_call x1, Pallas kernels, per_device(): pl.pallas_call(functools.partial(place_kernel, n_stream, n_span), name='p...  4.53 us
    unnamed x6, local copies, waits for them, and re-layouts  1.07 us

profile of v7, /device:TPU:7, one launch (start us, length us, event | category | flops | bytes accessed | tf_op | source)
XLA Modules:
  0.0 32.1 jit_solution(435021364863168031)
XLA Ops:
  0.0 0.0 copy-start
  0.0 12.7 %exchange.1 = (f32[5120,128]{1,0:T(8,128)S(1)}, f32[21,40,128]{2,1,0:T(8,128)S(1)}) custom-call(s32[32,1,128]{2,1,0:T(1,128)} %bitcast.5, f32[3,32,128]{2,1,0:T(8,128)} %bitcast.4, f32[5,16,32,128]{3,2,1,0:T(8,128)} %now_hbm.1, f32[5,16,32,128]{3,2,1,0:T(8,128)} %prev_hbm.1), custom_call_target="tpu_custom_call" | custom-call | tf_op jit(solution)/shard_map/exchange/pallas_call | solution.py:625
  12.8 0.0 copy-done
  12.8 0.0 copy-start.1
  12.8 4.5 %place.1 = (f32[5,16,32,128]{3,2,1,0:T(8,128)S(1)}, f32[5,16,32,128]{3,2,1,0:T(8,128)S(1)}) custom-call(s32[32,1,128]{2,1,0:T(1,128)S(1)} %bitcast.3, f32[5120,128]{1,0:T(8,128)S(1)} %get-tuple-element.9.packed_hbm, f32[21,40,128]{2,1,0:T(8,128)S(1)} %get-tuple-element.10.fresh_ref), custom_call_target="tpu_custom_call" | custom-call | tf_op jit(solution)/shard_map/place/pallas_call | solution.py:651
  17.3 0.0 copy-done.1
  17.3 0.1 reshape.12.jac
  17.4 13.6 %advance.1 = f32[5,16,32,128]{3,2,1,0:T(8,128)S(1)} custom-call(f32[75]{0:T(128)S(1)} %reshape.12.jac, f32[5,16,32,128]{3,2,1,0:T(8,128)S(1)} %get-tuple-element.11.q_hbm, f32[5,16,32,128]{3,2,1,0:T(8,128)S(1)} %get-tuple-element.12.old_ref), custom_call_target="tpu_custom_call" | custom-call | tf_op jit(solution)/shard_map/advance/pallas_call | solution.py:664
  31.1 1.1 %copy.10 = f32[5,16,32,128]{3,2,1,0:T(8,128)} copy(f32[5,16,32,128]{3,2,1,0:T(8,128)S(1)} %advance.1) | data formatting | bytes 2621440
  (1 shorter events, 0.0 us)
Async XLA Ops:
  0.0 12.8 %copy-start = (s32[1,4096]{1,0:T(1,128)S(1)}, s32[1,4096]{1,0:T(1,128)}, u32[]{:S(2)}) copy-start(s32[1,4096]{1,0:T(1,128)} %param.11) | copy-start | bytes 49156
  12.8 4.5 %copy-start.1 = (f32[3,5,5]{2,0,1:T(4,128)S(1)}, f32[3,5,5]{2,0,1:T(4,128)}, u32[]{:S(2)}) copy-start(f32[3,5,5]{2,0,1:T(4,128)} %param.8) | copy-start | bytes 904
